TPU v7x, 128 devices: a whole 4x4x4 slice. The times are simulated.
128 devices in a mesh: node: 16 (over y_hi, z, core), local: 8 (over x, y_lo).
Axes of the slice: x: 4, y: 4 (y_hi: 2, y_lo: 2; y = y_hi * 2 + y_lo), z: 4, core: 2. Of those that a mesh axis runs over, the one named last changes fastest.
Arguments:
- heads_out: bfloat16 [16384, 4096], P(('node', 'local')), may hold values from -24 to 24
- residual: bfloat16 [16384, 8192], P(('node', 'local')), may hold values from -6 to 6
- out_proj: bfloat16 [4096, 8192], P('node', 'local'), may hold values from -0.09375 to 0.09375
- cotangent: bfloat16 [16384, 8192], P(('node', 'local')), may hold values from -24 to 24
Outputs:
- layer_out: bfloat16 [16384, 8192], P(('node', 'local'))
- grad_heads: bfloat16 [16384, 4096], P(('node', 'local'))
- grad_proj: bfloat16 [4096, 8192], P('node', 'local')
All inputs are finite; a program needn't handle non-finite values.
Results may differ from a plain program's by a relative error of at most 0.025.
Values may be sent and summed in bfloat16 or wider, within the bound.
No kernel may reach another device: no remote copies, remote signals or barrier semaphores. Data moves between devices by JAX's collectives and lax.ppermute only.
A program may use at most 128 MiB of HBM per device.

v0:
```python
import jax
import jax.numpy as jnp
from jax import lax
from jax.sharding import PartitionSpec as P


def per_device(heads_out, residual, out_proj, cotangent):
    node_heads = lax.all_gather(heads_out, "local", axis=0, tiled=True)
    cot_columns = lax.all_to_all(cotangent, "local", split_axis=1, concat_axis=0, tiled=True)
    feature_block = node_heads
    projected = jnp.dot(
        feature_block,
        lax.all_gather(out_proj, "node", axis=0, tiled=True),
        preferred_element_type=jnp.float32,
    )
    proj_columns = lax.all_gather(out_proj, "node", axis=0, tiled=True)
    token_proj = lax.all_to_all(
        projected.astype(jnp.bfloat16), "local", split_axis=0, concat_axis=1, tiled=True
    )
    layer_out = (residual.astype(jnp.float32) + token_proj.astype(jnp.float32)).astype(jnp.bfloat16)
    grad_heads = lax.psum_scatter(
        lax.dot_general(
            cot_columns, proj_columns, (((1,), (1,)), ((), ())), preferred_element_type=jnp.float32
        ).astype(jnp.bfloat16),
        "local",
        scatter_dimension=0,
        tiled=True,
    )
    factor = 1.0 / jnp.sqrt(jnp.float32(node_heads.shape[0] * lax.axis_size("node")))
    feature_block = node_heads
    product = lax.dot_general(
        feature_block, cot_columns, (((0,), (0,)), ((), ())), preferred_element_type=jnp.float32
    )
    grad_proj = lax.psum_scatter(
        (product * factor).astype(jnp.bfloat16), "node", scatter_dimension=0, tiled=True
    )
    return (layer_out, grad_heads, grad_proj)


def solution(mesh):
    placed = (
        P(("node", "local"), None),
        P(("node", "local"), None),
        P("node", "local"),
        P(("node", "local"), None),
    )
    return jax.shard_map(
        per_device,
        mesh=mesh,
        in_specs=placed,
        out_specs=(P(("node", "local"), None), P(("node", "local"), None), P("node", "local")),
        check_vma=False,
    )
```

profile of v0, /device:TPU:1, one launch (start us, length us, event | category | flops | bytes accessed | tf_op | source)
XLA Modules:
  0.0 582.1 jit_solution(13896863443027815531)
XLA Ops:
  7.2 0.0 all-gather.3.cloned.1.call-start
  7.2 0.7 all-gather.3.cloned.1.call-update
  7.9 0.0 all-gather.5.cloned.1.call-start
  7.9 0.7 all-gather.5.cloned.1.call-update
  8.6 0.0 reduce-scatter.5.cloned.1.call-start
  8.7 4.1 copy.10
  12.8 44.4 %all_to_all.32 = bf16[128,8,1024]{0,2,1:T(8,128)(2,1)S(1)} all-to-all(bf16[128,8,1024]{0,2,1:T(8,128)(2,1)} %bitcast.16), channel_id=1, replica_groups=mesh['node'=16,'local'=8] {'local'}, dimensions={1} | all-to-all | bytes 4194304 | tf_op jit(solution)/shard_map/all_to_all | solution.py:9
  57.2 2.6 copy.11
  59.8 142.0 %all-gather.3.cloned.1.call-done = bf16[1024,4096]{1,0:T(8,128)(2,1)} async-done(((bf16[128,4096]{1,0:T(8,128)(2,1)}), bf16[1024,4096]{1,0:T(8,128)(2,1)}) %all-gather.3.cloned.1.call-update) | async-done | bytes 8388624 | tf_op jit(solution)/shard_map/all_gather | solution.py:8
  201.8 14.9 %multiply_convert_fusion = bf16[4096,1024]{1,0:T(8,128)(2,1)} fusion(bf16[1024,4096]{1,0:T(8,128)(2,1)} %all-gather.3.cloned.1.call-done, bf16[1024,1024]{1,0:T(8,128)(2,1)} %bitcast.17), kind=kOutput, calls=%fused_computation | convolution fusion | flops 8598323200 | bytes 18874368 | tf_op jit(solution)/shard_map/dot_general | solution.py:31
  216.7 0.0 copy-start
  216.7 0.0 reduce-scatter.5.cloned.1.call-update
  216.7 0.0 reduce-scatter.3.cloned.1.call-start
  216.8 67.3 %all-gather.5.cloned.1.call-done = bf16[4096,1024]{1,0:T(8,128)(2,1)} async-done(((bf16[256,1024]{1,0:T(8,128)(2,1)}), bf16[4096,1024]{1,0:T(8,128)(2,1)}) %all-gather.5.cloned.1.call-update) | async-done | bytes 8388624 | tf_op jit(solution)/shard_map/all_gather | solution.py:13
  284.1 0.0 copy-done
  284.1 14.3 %convolution_convert_fusion = bf16[1024,4096]{1,0:T(8,128)(2,1)} fusion(bf16[1024,1024]{1,0:T(8,128)(2,1)S(1)} %bitcast.18, bf16[4096,1024]{1,0:T(8,128)(2,1)} %all-gather.5.cloned.1.call-done), kind=kOutput, calls=%fused_computation.1 | convolution fusion | flops 8594128896 | bytes 18874368 | tf_op jit(solution)/shard_map/dot_general | solution.py:22
  298.4 0.0 reduce-scatter.3.cloned.1.call-update
  298.4 14.9 %convolution_convert_fusion.1 = bf16[1024,1024]{1,0:T(8,128)(2,1)S(1)} fusion(bf16[1024,4096]{1,0:T(8,128)(2,1)} %all-gather.3.cloned.1.call-done, bf16[4096,1024]{1,0:T(8,128)(2,1)} %all-gather.5.cloned.1.call-done), kind=kOutput, calls=%fused_computation.4 | convolution fusion | flops 8590983168 | bytes 18874368 | tf_op jit(solution)/shard_map/dot_general | solution.py:11
  313.3 29.8 %all_to_all.33 = bf16[8,128,1024]{2,1,0:T(8,128)(2,1)S(1)} all-to-all(bf16[8,128,1024]{2,1,0:T(8,128)(2,1)S(1)} %bitcast.19), channel_id=1, replica_groups=mesh['node'=16,'local'=8] {'local'}, dimensions={0} | all-to-all | bytes 4194304 | tf_op jit(solution)/shard_map/all_to_all | solution.py:17
  343.1 0.5 convert_bitcast_fusion
  343.6 0.0 copy-start.1
  343.6 0.3 copy.12
  343.9 1.3 copy-done.1
  345.2 1.8 add_convert_fusion
  347.0 56.9 %reduce-scatter.5.cloned.1.call-done = bf16[256,1024]{1,0:T(8,128)(2,1)} async-done(((bf16[4096,1024]{1,0:T(8,128)(2,1)}), bf16[256,1024]{1,0:T(8,128)(2,1)}) %reduce-scatter.5.cloned.1.call-update) | async-done | bytes 524304 | tf_op jit(solution)/shard_map/reduce_scatter | solution.py:34
  403.9 171.7 %reduce-scatter.3.cloned.1.call-done = bf16[128,4096]{1,0:T(8,128)(2,1)} async-done(((bf16[1024,4096]{1,0:T(8,128)(2,1)}), bf16[128,4096]{1,0:T(8,128)(2,1)}) %reduce-scatter.3.cloned.1.call-update) | async-done | bytes 1048592 | tf_op jit(solution)/shard_map/reduce_scatter | solution.py:21
Async XLA Ops:
  7.2 194.6 %all-gather.3.cloned.1.call-start = ((), (), s32[]{:S(2)}) async-start(), calls=%async_computation.4 | async-start | bytes 9437184 | tf_op jit(solution)/shard_map/all_gather | solution.py:8
  7.9 276.2 %all-gather.5.cloned.1.call-start = ((), (), s32[]{:S(2)}) async-start(), calls=%async_computation.5 | async-start | bytes 8912896 | tf_op jit(solution)/shard_map/all_gather | solution.py:13
  8.6 395.2 %reduce-scatter.5.cloned.1.call-start = ((), (), s32[]{:S(2)}) async-start(), calls=%async_computation.7 | async-start | bytes 8912896 | tf_op jit(solution)/shard_map/reduce_scatter | solution.py:34
  216.7 67.4 %copy-start = (bf16[8,128,1024]{2,1,0:T(8,128)(2,1)S(1)}, bf16[8,128,1024]{2,1,0:T(8,128)(2,1)}, u32[]{:S(2)}) copy-start(bf16[8,128,1024]{2,1,0:T(8,128)(2,1)} %copy.11) | copy-start | bytes 6291460
  216.7 358.9 %reduce-scatter.3.cloned.1.call-start = ((), (), s32[]{:S(2)}) async-start(), calls=%async_computation.6 | async-start | bytes 9437184 | tf_op jit(solution)/shard_map/reduce_scatter | solution.py:21
  343.6 1.6 copy-start.1
Sparse Core Ops, SparseCore 0:
  9.6 192.1 all-gather.2
  204.3 79.7 all-gather.4
  288.9 114.8 reduce-scatter.4
  406.7 168.8 reduce-scatter.2
where the time goes:
time: 582 us
  waiting for transfers between devices  439 us (75%)
  blocking collectives  74.2 us (13%)
  matrix products  44.1 us (8%)
  between operations  13.8 us (2%)
  local copies, waits for them, and re-layouts  8.24 us (1%)
    reduce_scatter x1, waiting for transfers between devices, per_device(): lax.psum_scatter(lax.dot_general(cot_columns, proj_columns, (((1,), (1,))...  172 us
    all_gather x1, waiting for transfers between devices, per_device(): node_heads = lax.all_gather(heads_out, 'local', axis=0, tiled=True)  142 us
    all_gather x1, waiting for transfers between devices, per_device(): lax.all_gather(out_proj, 'node', axis=0, tiled=True)  67.3 us
    reduce_scatter x1, waiting for transfers between devices, per_device(): lax.psum_scatter((product * factor).astype(jnp.bfloat16), 'node', scatter...  56.9 us
    all_to_all x1, blocking collectives, per_device(): lax.all_to_all(cotangent, 'local', split_axis=1, concat_axis=0, tiled=True)  44.4 us
    all_to_all x1, blocking collectives, per_device(): lax.all_to_all(projected.astype(jnp.bfloat16), 'local', split_axis=0, con...  29.8 us
    dot_general x1, matrix products, per_device(): lax.dot_general(feature_block, cot_columns, (((0,), (0,)), ((), ())), pre...  14.9 us
    dot_general x1, matrix products, per_device(): jnp.dot(feature_block, lax.all_gather(out_proj, 'node', axis=0, tiled=Tru...  14.9 us
  transfers between devices with their start and end apart: 4, of which 4 were waited for; matrix products, arithmetic and copies ran while one was open for 9% of the time, Pallas kernels for 0%

commit v1 on v0

v1 whole, which is shorter than its diff:
```python
import jax
import jax.numpy as jnp
from jax import lax
from jax.sharding import Mesh, PartitionSpec as P

AXES = ("yh", "z", "c", "x", "yl")
GROUP = ("x", "c")
ROWS = ("yh", "z", "yl")


def swap(block):
    pairs = []
    for yh in range(2):
        for z in range(4):
            for c in range(2):
                for x in range(4):
                    for yl in range(2):
                        here = (((yh * 4 + z) * 2 + c) * 4 + x) * 2 + yl
                        there = (((yh * 4 + z) * 2 + yl) * 4 + x) * 2 + c
                        pairs.append((here, there))
    return lax.ppermute(block, AXES, pairs)


def per_device(heads_out, residual, out_proj, cotangent):
    heads = lax.all_gather(heads_out, GROUP, axis=0, tiled=True)
    proj = lax.all_gather(swap(out_proj), ROWS, axis=0, tiled=True)
    cot = lax.all_to_all(cotangent, GROUP, split_axis=1, concat_axis=0, tiled=True)
    factor = 1.0 / jnp.sqrt(jnp.float32(heads.shape[0] * lax.axis_size(ROWS)))
    product = lax.dot_general(heads, cot, (((0,), (0,)), ((), ())), preferred_element_type=jnp.float32)
    grad_proj = swap(
        lax.psum_scatter((product * factor).astype(jnp.bfloat16), ROWS, scatter_dimension=0, tiled=True)
    )
    act = lax.dot_general(cot, proj, (((1,), (1,)), ((), ())), preferred_element_type=jnp.float32)
    grad_heads = lax.psum_scatter(act.astype(jnp.bfloat16), GROUP, scatter_dimension=0, tiled=True)
    projected = jnp.dot(heads, proj, preferred_element_type=jnp.float32).astype(jnp.bfloat16)
    token_proj = lax.all_to_all(projected, GROUP, split_axis=0, concat_axis=1, tiled=True)
    layer_out = (residual.astype(jnp.float32) + token_proj.astype(jnp.float32)).astype(jnp.bfloat16)
    return (layer_out, grad_heads, grad_proj)


def solution(mesh):
    fine = Mesh(mesh.devices.reshape(2, 4, 2, 4, 2), AXES)
    tokens, grid = P(AXES, None), P(("yh", "z", "c"), ("x", "yl"))
    return jax.shard_map(
        per_device,
        mesh=fine,
        in_specs=(tokens, tokens, grid, tokens),
        out_specs=(tokens, tokens, grid),
        check_vma=False,
    )
```

time: 582 us -> 515 us (0.88)
  waiting for transfers between devices: 439 us -> 349 us
  blocking collectives: 74.2 us -> 84.9 us
  starting transfers between devices: 0.16 us -> 8.41 us
    reduce_scatter x2, waiting for transfers between devices: 229 us -> 166 us  [the longest x1 121 us: per_device(): lax.psum_scatter((product * factor).astype(jnp.bfloat16), ROWS, scatter_d...]
    all_gather x2, waiting for transfers between devices: 209 us -> 172 us  [the longest x1 167 us: per_device(): proj = lax.all_gather(swap(out_proj), ROWS, axis=0, tiled=True)]
    all_to_all x2, blocking collectives: 74.2 us -> 84.9 us  [the longest x1 53.5 us: per_device(): lax.all_to_all(cotangent, GROUP, split_axis=1, concat_axis=0, tiled=True)]
    ppermute x0 -> x2, waiting for transfers between devices: none -> 10.2 us  [swap(): return lax.ppermute(block, AXES, pairs)]
    ppermute x0 -> x2, starting transfers between devices: none -> 8.25 us  [swap(): return lax.ppermute(block, AXES, pairs)]
  transfers between devices with their start and end apart: 4 -> 6, of which waited for: 4 -> 6; matrix products, arithmetic and copies ran while one was open for 9% -> 11% of each run, Pallas kernels for 0% -> 0%
where the time goes in v1:
time: 515 us; the launch traced here: 514 us
  waiting for transfers between devices  349 us (68%)
  blocking collectives  84.9 us (16%)
  matrix products  42.9 us (8%)
  between operations  13.8 us (3%)
  local copies, waits for them, and re-layouts  10.6 us (2%)
  starting transfers between devices  8.41 us (2%)
    all_gather x1, waiting for transfers between devices, per_device(): proj = lax.all_gather(swap(out_proj), ROWS, axis=0, tiled=True)  167 us
    reduce_scatter x1, waiting for transfers between devices, per_device(): lax.psum_scatter((product * factor).astype(jnp.bfloat16), ROWS, scatter_d...  121 us
    all_to_all x1, blocking collectives, per_device(): lax.all_to_all(cotangent, GROUP, split_axis=1, concat_axis=0, tiled=True)  53.5 us
    reduce_scatter x1, waiting for transfers between devices, per_device(): lax.psum_scatter(act.astype(jnp.bfloat16), GROUP, scatter_dimension=0, ti...  45 us
    all_to_all x1, blocking collectives, per_device(): lax.all_to_all(projected, GROUP, split_axis=0, concat_axis=1, tiled=True)  31.4 us
    dot_general x1, matrix products, per_device(): lax.dot_general(heads, cot, (((0,), (0,)), ((), ())), preferred_element_t...  14.9 us
    dot_general x1, matrix products, per_device(): lax.dot_general(cot, proj, (((1,), (1,)), ((), ())), preferred_element_ty...  14.3 us
    dot_general x1, matrix products, per_device(): jnp.dot(heads, proj, preferred_element_type=jnp.float32)  13.7 us
  transfers between devices with their start and end apart: 6, of which 6 were waited for; matrix products, arithmetic and copies ran while one was open for 11% of the time, Pallas kernels for 0%

profile of v1, /device:TPU:1, one launch (start us, length us, event | category | flops | bytes accessed | tf_op | source)
XLA Modules:
  0.0 514.1 jit_solution(4876669143420214496)
XLA Ops:
  7.2 0.0 all-gather.3.cloned.1.call-start
  7.2 0.7 all-gather.3.cloned.1.call-update
  7.9 0.0 all-gather.5.cloned.1.call-start
  7.9 4.6 collective-permute-start
  12.5 7.1 %collective-permute-done = bf16[256,1024]{1,0:T(8,128)(2,1)S(1)} collective-permute-done((bf16[256,1024]{1,0:T(8,128)(2,1)}, bf16[256,1024]{1,0:T(8,128)(2,1)S(1)}, u32[]{:S(2)}, u32[]{:S(2)}) %collective-permute-start) | collective-permute-done | bytes 524320 | tf_op jit(solution)/shard_map/ppermute | solution.py:21
  19.6 0.0 copy-start.2
  19.6 0.8 copy-done.2
  20.4 0.0 all-gather.5.cloned.1.call-update
  20.4 0.0 reduce-scatter.5.cloned.1.call-start
  20.5 4.2 copy.10
  24.6 53.5 %all_to_all.32 = bf16[128,8,1024]{0,2,1:T(8,128)(2,1)S(1)} all-to-all(bf16[128,8,1024]{0,2,1:T(8,128)(2,1)} %bitcast.16), channel_id=1, replica_groups=mesh['yh'=2,'z'=4,'c'=2,'x'=4,'yl'=2] {'x','c'}, dimensions={1} | all-to-all | bytes 4194304 | tf_op jit(solution)/shard_map/all_to_all | solution.py:27
  78.1 2.6 copy.11
  80.7 4.9 all-gather.3.cloned.1.call-done
  85.5 14.9 %multiply_convert_fusion = bf16[4096,1024]{1,0:T(8,128)(2,1)} fusion(bf16[1024,4096]{1,0:T(8,128)(2,1)} %all-gather.3.cloned.1.call-done, bf16[1024,1024]{1,0:T(8,128)(2,1)} %bitcast.17), kind=kOutput, calls=%fused_computation | convolution fusion | flops 8598323200 | bytes 18874368 | tf_op jit(solution)/shard_map/dot_general | solution.py:29
  100.4 0.0 copy-start
  100.4 0.0 reduce-scatter.5.cloned.1.call-update
  100.5 0.0 reduce-scatter.3.cloned.1.call-start
  100.5 167.0 %all-gather.5.cloned.1.call-done = bf16[4096,1024]{1,0:T(8,128)(2,1)} async-done(((bf16[256,1024]{1,0:T(8,128)(2,1)}), bf16[4096,1024]{1,0:T(8,128)(2,1)}) %all-gather.5.cloned.1.call-update) | async-done | bytes 8388624 | tf_op jit(solution)/shard_map/all_gather | solution.py:26
  267.5 0.0 copy-done
  267.5 14.3 %convolution_convert_fusion = bf16[1024,4096]{1,0:T(8,128)(2,1)} fusion(bf16[1024,1024]{1,0:T(8,128)(2,1)S(1)} %bitcast.18, bf16[4096,1024]{1,0:T(8,128)(2,1)} %all-gather.5.cloned.1.call-done), kind=kOutput, calls=%fused_computation.1 | convolution fusion | flops 8594128896 | bytes 18874368 | tf_op jit(solution)/shard_map/dot_general | solution.py:33
  281.8 0.0 reduce-scatter.3.cloned.1.call-update
  281.8 13.7 %convolution_convert_fusion.1 = bf16[1024,1024]{1,0:T(8,128)(2,1)S(1)} fusion(bf16[1024,4096]{1,0:T(8,128)(2,1)} %all-gather.3.cloned.1.call-done, bf16[4096,1024]{1,0:T(8,128)(2,1)} %all-gather.5.cloned.1.call-done), kind=kOutput, calls=%fused_computation.4 | convolution fusion | flops 8590983168 | bytes 18874368 | tf_op jit(solution)/shard_map/dot_general | solution.py:35
  295.5 31.4 %all_to_all.33 = bf16[8,128,1024]{2,1,0:T(8,128)(2,1)S(1)} all-to-all(bf16[8,128,1024]{2,1,0:T(8,128)(2,1)S(1)} %bitcast.19), channel_id=1, replica_groups=mesh['yh'=2,'z'=4,'c'=2,'x'=4,'yl'=2] {'x','c'}, dimensions={0} | all-to-all | bytes 4194304 | tf_op jit(solution)/shard_map/all_to_all | solution.py:36
  326.9 0.5 convert_bitcast_fusion
  327.4 0.0 copy-start.1
  327.4 2.3 copy.12
  329.6 121.5 %reduce-scatter.5.cloned.1.call-done = bf16[256,1024]{1,0:T(8,128)(2,1)} async-done(((bf16[4096,1024]{1,0:T(8,128)(2,1)}), bf16[256,1024]{1,0:T(8,128)(2,1)}) %reduce-scatter.5.cloned.1.call-update) | async-done | bytes 524304 | tf_op jit(solution)/shard_map/reduce_scatter | solution.py:31
  451.1 3.7 collective-permute-start.1
  454.8 0.0 copy-done.1
  454.8 3.9 add_convert_fusion
  458.7 3.1 collective-permute-done.1
  461.8 45.0 %reduce-scatter.3.cloned.1.call-done = bf16[128,4096]{1,0:T(8,128)(2,1)} async-done(((bf16[1024,4096]{1,0:T(8,128)(2,1)}), bf16[128,4096]{1,0:T(8,128)(2,1)}) %reduce-scatter.3.cloned.1.call-update) | async-done | bytes 1048592 | tf_op jit(solution)/shard_map/reduce_scatter | solution.py:34
  506.8 0.8 copy.14
Async XLA Ops:
  7.2 78.4 %all-gather.3.cloned.1.call-start = ((), (), s32[]{:S(2)}) async-start(), calls=%async_computation.4 | async-start | bytes 9437184 | tf_op jit(solution)/shard_map/all_gather | solution.py:25
  7.9 259.6 %all-gather.5.cloned.1.call-start = ((), (), s32[]{:S(2)}) async-start(), calls=%async_computation.5 | async-start | bytes 8912896 | tf_op jit(solution)/shard_map/all_gather | solution.py:26
  7.9 11.7 %collective-permute-start = (bf16[256,1024]{1,0:T(8,128)(2,1)}, bf16[256,1024]{1,0:T(8,128)(2,1)S(1)}, u32[]{:S(2)}, u32[]{:S(2)}) collective-permute-start(bf16[256,1024]{1,0:T(8,128)(2,1)} %param.6), channel_id=1, source_target_pairs={{0,0},{1,8},{2,2},{3,10},{4,4},{5,12},{6,6},{7,14},{8,1},{9,9},{10... | collective-permute-start | bytes 1572872 | tf_op jit(solution)/shard_map/ppermute | solution.py:21
  19.6 0.8 copy-start.2
  20.4 430.7 %reduce-scatter.5.cloned.1.call-start = ((), (), s32[]{:S(2)}) async-start(), calls=%async_computation.7 | async-start | bytes 8912896 | tf_op jit(solution)/shard_map/reduce_scatter | solution.py:31
  100.4 167.0 %copy-start = (bf16[8,128,1024]{2,1,0:T(8,128)(2,1)S(1)}, bf16[8,128,1024]{2,1,0:T(8,128)(2,1)}, u32[]{:S(2)}) copy-start(bf16[8,128,1024]{2,1,0:T(8,128)(2,1)} %copy.11) | copy-start | bytes 6291460
  100.5 406.4 %reduce-scatter.3.cloned.1.call-start = ((), (), s32[]{:S(2)}) async-start(), calls=%async_computation.6 | async-start | bytes 9437184 | tf_op jit(solution)/shard_map/reduce_scatter | solution.py:34
  327.4 127.4 %copy-start.1 = (bf16[128,8192]{1,0:T(8,128)(2,1)S(1)}, bf16[128,8192]{1,0:T(8,128)(2,1)}, u32[]{:S(2)}) copy-start(bf16[128,8192]{1,0:T(8,128)(2,1)} %param.5) | copy-start | bytes 6291460
  451.1 10.7 %collective-permute-start.1 = (bf16[256,1024]{1,0:T(8,128)(2,1)}, bf16[256,1024]{1,0:T(8,128)(2,1)S(1)}, u32[]{:S(2)}, u32[]{:S(2)}) collective-permute-start(bf16[256,1024]{1,0:T(8,128)(2,1)} %reduce-scatter.5.cloned.1.call-done), channel_id=1, source_target_pairs={{0,0},{1,8},{2,2},{3,10},{4,4},{5,12},{6,6},{7,14},{8,1},{9,9},{10... | collective-permute-start | bytes 1572872 | tf_op jit(solution)/shard_map/ppermute | solution.py:21
Sparse Core Ops, SparseCore 0:
  9.7 75.7 all-gather.2
  87.8 179.6 all-gather.4
  269.9 181.1 reduce-scatter.4
  453.9 52.8 reduce-scatter.2

commit v2 on v1

v2 whole, which is shorter than its diff:
```python
import functools

import jax
import jax.numpy as jnp
from jax import lax
from jax.experimental import pallas as pl
from jax.experimental.pallas import tpu as pltpu
from jax.sharding import Mesh, PartitionSpec as P

AXES = ("yh", "z", "c", "x", "yl")
BF16, F32 = jnp.bfloat16, jnp.float32
WIDE = 1024


def flat(x, y, z, c):
    return ((((y // 2) * 4 + z) * 2 + c) * 4 + x) * 2 + y % 2


def moves(to):
    pairs = []
    for x in range(4):
        for y in range(4):
            for z in range(4):
                for c in range(2):
                    pairs.append((flat(x, y, z, c), flat(*to(x, y, z, c))))
    return sorted(pairs)


X_AHEAD = moves(lambda x, y, z, c: ((x + 1 + 2 * c) % 4, y, z, c))
X_BACK = moves(lambda x, y, z, c: ((x + 3 + 2 * c) % 4, y, z, c))
Y_AHEAD = moves(lambda x, y, z, c: (x, (y + 1 + 2 * c) % 4, z, c))
Y_BACK = moves(lambda x, y, z, c: (x, (y + 3 + 2 * c) % 4, z, c))
Z_AHEAD = moves(lambda x, y, z, c: (x, y, (z + 1 + 2 * c) % 4, c))
Z_BACK = moves(lambda x, y, z, c: (x, y, (z + 3 + 2 * c) % 4, c))
X_ACROSS = moves(lambda x, y, z, c: ((x + 2) % 4, y, z, c))
CORE = moves(lambda x, y, z, c: (x, y, z, 1 - c))
SWAP = moves(lambda x, y, z, c: (x, y - y % 2 + c, z, y % 2))


def add(*terms):
    return functools.reduce(lambda p, q: p + q, [t.astype(F32) for t in terms]).astype(BF16)


def feature_block(k, y, z):
    part, far = k // 16, (k % 16) // 4
    dy, dz = (k % 4, far) if part == 0 else (far, k % 4)
    yy, zz = (y + 4 - dy) % 4, (z + 4 - dz) % 4
    return (yy // 2) * 16 + zz * 4 + (yy % 2) * 2 + part


def ordered_kernel(place, heads, out):
    for k in range(32):
        at = pl.multiple_of(feature_block(k, place[1], place[2]) * 128, 128)
        out[:, k * 128 : (k + 1) * 128] = heads[:, pl.ds(at, 128)]


def restored_kernel(place, grad, out):
    for k in range(32):
        at = pl.multiple_of(feature_block(k, place[1], place[2]) * 128, 128)
        out[:, pl.ds(at, 128)] = grad[:, k * 128 : (k + 1) * 128]


def columns_kernel(place, cotangent, here, ahead, back, across):
    x, c = place[0], place[3]
    step = 1 + 2 * c
    for distance, out in ((0, here), (step, ahead), (4 - step, back), (2, across)):
        for e in range(2):
            at = pl.multiple_of(((x + distance) % 4 * 2 + (c + e) % 2) * WIDE, WIDE)
            out[e] = cotangent[:, pl.ds(at, WIDE)]


def tokens_kernel(place, here, ahead, back, across, given, out):
    x, c = place[0], place[3]
    step = 1 + 2 * c
    n = here.shape[1]
    for e, (distance, piece) in enumerate(((0, here), (4 - step, ahead), (2, across), (step, back))):
        at = (x + distance) % 4 * 2
        out[pl.ds(pl.multiple_of((at + c) * n, n), n), :] = piece[0]
    for e, distance in enumerate((0, step, 2, 4 - step)):
        at = (x + distance) % 4 * 2
        out[pl.ds(pl.multiple_of((at + 1 - c) * n, n), n), :] = given[e * n : (e + 1) * n, :]


def outgoing_kernel(place, own, got, here, ahead, back, across):
    x, c = place[0], place[3]
    step = 1 + 2 * c
    for distance, out in ((0, here), (step, ahead), (4 - step, back), (2, across)):
        out[0] = own[(x + distance) % 4]
        out[1] = got[(x + distance) % 4]


def layer_kernel(place, residual, here, ahead, back, across, out):
    x, c = place[0], place[3]
    step = 1 + 2 * c
    pieces = []
    for distance, both in ((0, here), (4 - step, ahead), (step, back), (2, across)):
        pieces += [(x + distance, c, both.at[0]), (x + distance, 1 - c, both.at[1])]
    for xx, cc, piece in pieces:
        at = pl.multiple_of((xx % 4 * 2 + cc) * WIDE, WIDE)
        total = residual[:, pl.ds(at, WIDE)].astype(F32) + piece[...].astype(F32)
        out[:, pl.ds(at, WIDE)] = total.astype(BF16)


def local(kernel, shapes, place, *operands):
    vmem = pl.BlockSpec(memory_space=pltpu.VMEM)
    return pl.pallas_call(
        kernel,
        out_shape=jax.tree.map(lambda s: jax.ShapeDtypeStruct(s, BF16), shapes, is_leaf=lambda s: isinstance(s[0], int)),
        in_specs=[pl.BlockSpec(memory_space=pltpu.SMEM)] + [vmem] * len(operands),
        out_specs=jax.tree.map(lambda s: vmem, shapes, is_leaf=lambda s: isinstance(s[0], int)),
        compiler_params=pltpu.CompilerParams(vmem_limit_bytes=24 * 1024 * 1024),
    )(place, *operands)


def dot(a, b, dims):
    return lax.dot_general(a, b, (dims, ((), ())), preferred_element_type=F32)


class Line:
    def __init__(self):
        self.token = jnp.zeros((), jnp.int32)

    def wait(self, *values):
        self.token, *values = lax.optimization_barrier((self.token, *values))
        return values[0] if len(values) == 1 else values

    def send(self, value, pairs):
        return lax.ppermute(self.wait(value), AXES, pairs)


def per_device(heads_out, residual, out_proj, cotangent):
    x, c = lax.axis_index("x"), lax.axis_index("c")
    y, z = 2 * lax.axis_index("yh") + lax.axis_index("yl"), lax.axis_index("z")
    place = jnp.stack([x, y, z, c]).astype(jnp.int32)
    first = c == 0
    n = heads_out.shape[0]
    line = Line()
    send, wait = line.send, line.wait

    def pick(ahead, back):
        return jnp.where(first, ahead, back), jnp.where(first, back, ahead)

    def ring(zero, ahead, far, back):
        one, three = pick(ahead, back)
        return jnp.concatenate([zero, one, far, three])

    mine = send(out_proj, SWAP)
    ordered = local(ordered_kernel, heads_out.shape, place, heads_out)
    heads = lax.all_gather(ordered, ("x", "c"), axis=0, tiled=True)
    pair = (2, n, WIDE)
    cot_here, ahead, back, across = local(columns_kernel, (pair, pair, pair, pair), place, cotangent)
    cot_ahead = send(ahead, X_AHEAD)
    cot_back = send(back, X_BACK)
    cot_across = send(across, X_ACROSS)
    mine = wait(mine)
    half = mine.shape[0] // 2
    up, lo = mine[:half], mine[half:]
    up_ahead = send(up, Y_AHEAD)
    lo_ahead = send(lo, Z_AHEAD)
    up_ahead = wait(up_ahead)
    up_back = send(up, Y_BACK)
    lo_ahead = wait(lo_ahead)
    lo_back = send(lo, Z_BACK)
    cot_ahead = wait(cot_ahead)
    up_far = send(up_ahead, Y_AHEAD)
    cot_back = wait(cot_back)
    lo_far = send(lo_ahead, Z_AHEAD)
    up_back, up_far = wait(up_back, up_far)
    up = ring(up, up_ahead, up_far, up_back)
    up_ahead = send(up, Z_AHEAD)
    lo_back, lo_far = wait(lo_back, lo_far)
    lo = ring(lo, lo_ahead, lo_far, lo_back)
    lo_ahead = send(lo, Y_AHEAD)
    up_back = send(up, Z_BACK)
    lo_back = send(lo, Y_BACK)
    cot_across = wait(cot_across)
    cot_given = send(jnp.concatenate([cot_here[1], cot_ahead[1], cot_across[1], cot_back[1]]), CORE)
    cot_given = wait(cot_given)
    cot = local(
        tokens_kernel, (8 * n, WIDE), place, cot_here, cot_ahead, cot_back, cot_across, cot_given
    )
    up_ahead = wait(up_ahead)
    up_far = send(up_ahead, Z_AHEAD)
    lo_ahead = wait(lo_ahead)
    lo_far = send(lo_ahead, Y_AHEAD)
    up_back, lo_back = wait(up_back, lo_back)

    heads = wait(heads)
    factor = 1.0 / jnp.sqrt(jnp.float32(n * 128))

    def weight(k):
        return (dot(lax.dynamic_slice_in_dim(heads, k * 512, 512, 1), cot, ((0,), (0,))) * factor).astype(BF16)

    def row(block, d):
        m = block.shape[0] // 4
        return block[d * m : (d + 1) * m]

    one, three = jnp.where(first, 1, 3), jnp.where(first, 3, 1)
    sum_up_far = send(weight(2), Z_BACK)
    sum_lo_far = send(weight(6), Y_BACK)
    up_far, lo_far = wait(up_far, lo_far)
    sum_up_back = send(weight(three), Z_AHEAD)
    sum_lo_back = send(weight(4 + three), Y_AHEAD)
    proj = jnp.concatenate([ring(up, up_ahead, up_far, up_back), ring(lo, lo_ahead, lo_far, lo_back)])
    act = dot(cot, proj, ((1,), (1,))).astype(BF16)
    act = wait(act)
    grad_heads = lax.psum_scatter(act, ("x", "c"), scatter_dimension=0, tiled=True)
    weight_up, weight_lo = weight(one), weight(4 + one)
    sum_up_far = wait(sum_up_far)
    sum_up_ahead = send(add(weight_up, sum_up_far), Z_BACK)
    sum_lo_far = wait(sum_lo_far)
    sum_lo_ahead = send(add(weight_lo, sum_lo_far), Y_BACK)
    weight_up, weight_lo = wait(weight(0), weight(4))

    out = wait(dot(heads, proj, ((1,), (0,))).astype(BF16)).reshape(4, 2, n, WIDE)
    out_mine, out_given = [lax.dynamic_index_in_dim(out, e, 1, keepdims=False) for e in (c, 1 - c)]
    out_given = send(out_given, CORE)
    sum_up_back, sum_up_ahead = wait(sum_up_back, sum_up_ahead)
    up = add(weight_up, sum_up_ahead, sum_up_back)
    sum_up_far = send(row(up, 2), Y_BACK)
    sum_lo_back, sum_lo_ahead = wait(sum_lo_back, sum_lo_ahead)
    lo = add(weight_lo, sum_lo_ahead, sum_lo_back)
    sum_lo_far = send(row(lo, 2), Z_BACK)
    out_given = wait(out_given)
    out_here, ahead, back, across = local(outgoing_kernel, (pair, pair, pair, pair), place, out_mine, out_given)
    out_ahead = send(ahead, X_AHEAD)
    out_back = send(back, X_BACK)
    up_one, up_three = pick(row(up, 1), row(up, 3))
    lo_one, lo_three = pick(row(lo, 1), row(lo, 3))
    sum_up_back = send(up_three, Y_AHEAD)
    sum_up_far = wait(sum_up_far)
    sum_lo_back = send(lo_three, Z_AHEAD)
    sum_lo_far = wait(sum_lo_far)
    sum_up_ahead = send(add(up_one, sum_up_far), Y_BACK)
    sum_up_back = wait(sum_up_back)
    sum_lo_ahead = send(add(lo_one, sum_lo_far), Z_BACK)
    sum_lo_back = wait(sum_lo_back)
    out_across = send(across, X_ACROSS)
    sum_up_ahead, sum_lo_ahead = wait(sum_up_ahead, sum_lo_ahead)
    grad_proj = jnp.concatenate(
        [add(row(up, 0), sum_up_ahead, sum_up_back), add(row(lo, 0), sum_lo_ahead, sum_lo_back)]
    )
    grad_proj = send(grad_proj, SWAP)
    out_ahead, out_back, out_across = wait(out_ahead, out_back, out_across)
    layer_out = local(layer_kernel, residual.shape, place, residual, out_here, out_ahead, out_back, out_across)
    grad_heads = local(restored_kernel, heads_out.shape, place, grad_heads)
    return (layer_out, grad_heads, grad_proj)


def solution(mesh):
    fine = Mesh(mesh.devices.reshape(2, 4, 2, 4, 2), AXES)
    tokens, grid = P(AXES, None), P(("yh", "z", "c"), ("x", "yl"))
    return jax.shard_map(
        per_device,
        mesh=fine,
        in_specs=(tokens, tokens, grid, tokens),
        out_specs=(tokens, tokens, grid),
        check_vma=False,
    )
```

time: 515 us -> 223 us (0.43)
  waiting for transfers between devices: 349 us -> 93.7 us
  blocking collectives: 84.9 us -> 0 us
  starting transfers between devices: 8.41 us -> 51.4 us
  Pallas kernels: 0 us -> 9.06 us
  matrix products: 42.9 us -> 35.4 us
    all_gather x2 -> x1, waiting for transfers between devices: 172 us -> 0.02 us  [per_device(): heads = lax.all_gather(ordered, ('x', 'c'), axis=0, tiled=True)]
    reduce_scatter x2 -> x1, waiting for transfers between devices: 166 us -> 0.01 us  [per_device(): lax.psum_scatter(act, ('x', 'c'), scatter_dimension=0, tiled=True)]
    all_to_all x2 -> x0, blocking collectives: 84.9 us -> none  [the longest x1 53.5 us: per_device(): lax.all_to_all(cotangent, GROUP, split_axis=1, concat_axis=0, tiled=True)]
    ppermute x2 -> x34, waiting for transfers between devices: 10.2 us -> 93.7 us  [send(): return lax.ppermute(self.wait(value), AXES, pairs)]
    ppermute x2 -> x34, starting transfers between devices: 8.25 us -> 51.3 us  [send(): return lax.ppermute(self.wait(value), AXES, pairs)]
    pallas_call x0 -> x6, Pallas kernels: none -> 9.06 us  [local(): pl.pallas_call(kernel, out_shape=jax.tree.map(lambda s: jax.ShapeDtypeStr...]
    dot_general x3 -> x10, matrix products: 42.9 us -> 35.4 us  [dot(): return lax.dot_general(a, b, (dims, ((), ())), preferred_element_type=F32)]
  transfers between devices with their start and end apart: 6 -> 36, of which waited for: 6 -> 18; matrix products, arithmetic and copies ran while one was open for 11% -> 21% of each run, Pallas kernels for 0% -> 2%
where the time goes in v2:
time: 223 us; the launch traced here: 222 us
  waiting for transfers between devices  93.7 us (42%)
  starting transfers between devices  51.4 us (23%)
  matrix products  35.4 us (16%)
  between operations  14.6 us (7%)
  local copies, waits for them, and re-layouts  10.4 us (5%)
  Pallas kernels  9.06 us (4%)
  other arithmetic  7.28 us (3%)
    ppermute x34, waiting for transfers between devices, send(): return lax.ppermute(self.wait(value), AXES, pairs)  93.7 us
    ppermute x34, starting transfers between devices, send(): return lax.ppermute(self.wait(value), AXES, pairs)  51.3 us
    dot_general x10, matrix products, dot(): return lax.dot_general(a, b, (dims, ((), ())), preferred_element_type=F32)  35.4 us
    unnamed x40, local copies, waits for them, and re-layouts  9.29 us
    pallas_call x6, Pallas kernels, local(): pl.pallas_call(kernel, out_shape=jax.tree.map(lambda s: jax.ShapeDtypeStr...  9.06 us
  transfers between devices with their start and end apart: 36, of which 18 were waited for; matrix products, arithmetic and copies ran while one was open for 21% of the time, Pallas kernels for 2%

profile of v2, /device:TPU:1, one launch (start us, length us, event | category | flops | bytes accessed | tf_op | source)
XLA Modules:
  0.0 221.9 jit_solution(17389895111772352581)
XLA Ops:
  7.3 1.3 copy-done.6
  8.7 1.8 shard_map.68
  10.6 4.6 %collective-permute-start = (bf16[256,1024]{1,0:T(8,128)(2,1)S(1)}, bf16[256,1024]{1,0:T(8,128)(2,1)S(1)}, u32[]{:S(2)}, u32[]{:S(2)}) collective-permute-start(bf16[256,1024]{1,0:T(8,128)(2,1)S(1)} %copy-done.15), channel_id=1, source_target_pairs={{0,0},{1,8},{2,2},{3,10},{4,4},{5,12},{6,6},{7,14},{8,1},{9,9},{10... | collective-permute-start | bytes 1572872 | tf_op jit(solution)/shard_map/ppermute | solution.py:128
  15.2 1.7 shard_map.67
  16.8 2.5 %collective-permute-start.3 = (bf16[2,128,1024]{2,1,0:T(8,128)(2,1)S(1)}, bf16[2,128,1024]{2,1,0:T(8,128)(2,1)S(1)}, u32[]{:S(2)}, u32[]{:S(2)}) collective-permute-start(bf16[2,128,1024]{2,1,0:T(8,128)(2,1)S(1)} %get-tuple-element.134), channel_id=1, source_target_pairs={{0,2},{1,3},{2,4},{3,5},{4,6},{5,7},{6,0},{7,1},{8,14},{9,15},{10,... | collective-permute-start | bytes 1572872 | tf_op jit(solution)/shard_map/ppermute | solution.py:128
  19.3 3.0 %collective-permute-done = bf16[256,1024]{1,0:T(8,128)(2,1)S(1)} collective-permute-done((bf16[256,1024]{1,0:T(8,128)(2,1)S(1)}, bf16[256,1024]{1,0:T(8,128)(2,1)S(1)}, u32[]{:S(2)}, u32[]{:S(2)}) %collective-permute-start) | collective-permute-done | bytes 524320 | tf_op jit(solution)/shard_map/ppermute | solution.py:128
  23.2 3.8 %collective-permute-start.2 = (bf16[128,1024]{1,0:T(8,128)(2,1)S(1)}, bf16[128,1024]{1,0:T(8,128)(2,1)S(1)}, u32[]{:S(2)}, u32[]{:S(2)}) collective-permute-start(bf16[128,1024]{1,0:T(8,128)(2,1)S(1)} %get-tuple-element.148), channel_id=1, source_target_pairs={{0,16},{1,17},{2,18},{3,19},{4,20},{5,21},{6,22},{7,23},{8,56},{9,... | collective-permute-start | bytes 786440 | tf_op jit(solution)/shard_map/ppermute | solution.py:128
  26.9 2.7 %collective-permute-start.9 = (bf16[2,128,1024]{2,1,0:T(8,128)(2,1)}, bf16[2,128,1024]{2,1,0:T(8,128)(2,1)S(1)}, u32[]{:S(2)}, u32[]{:S(2)}) collective-permute-start(bf16[2,128,1024]{2,1,0:T(8,128)(2,1)} %get-tuple-element.156), channel_id=1, source_target_pairs={{0,4},{1,5},{2,6},{3,7},{4,0},{5,1},{6,2},{7,3},{8,12},{9,13},{10,... | collective-permute-start | bytes 1572872 | tf_op jit(solution)/shard_map/ppermute | solution.py:128
  30.3 7.0 %collective-permute-done.3.ahead = bf16[2,128,1024]{2,1,0:T(8,128)(2,1)S(1)} collective-permute-done((bf16[2,128,1024]{2,1,0:T(8,128)(2,1)S(1)}, bf16[2,128,1024]{2,1,0:T(8,128)(2,1)S(1)}, u32[]{:S(2)}, u32[]{:S(2)}) %collective-permute-start.3) | collective-permute-done | bytes 524320 | tf_op jit(solution)/shard_map/ppermute | solution.py:128
  37.3 1.5 collective-permute-start.5
  38.8 4.6 %collective-permute-start.8 = (bf16[128,1024]{1,0:T(8,128)(2,1)}, bf16[128,1024]{1,0:T(8,128)(2,1)S(1)}, u32[]{:S(2)}, u32[]{:S(2)}) collective-permute-start(bf16[128,1024]{1,0:T(8,128)(2,1)} %copy-done.11), channel_id=1, source_target_pairs={{0,16},{1,17},{2,18},{3,19},{4,20},{5,21},{6,22},{7,23},{8,56},{9,... | collective-permute-start | bytes 786440 | tf_op jit(solution)/shard_map/ppermute | solution.py:128
  43.4 1.8 collective-permute-done.6
  46.5 1.7 constant_dynamic-update-slice_fusion.7
  50.1 1.9 collective-permute-done.7
  52.2 5.9 %collective-permute-done.9.across = bf16[2,128,1024]{2,1,0:T(8,128)(2,1)S(1)} collective-permute-done((bf16[2,128,1024]{2,1,0:T(8,128)(2,1)}, bf16[2,128,1024]{2,1,0:T(8,128)(2,1)S(1)}, u32[]{:S(2)}, u32[]{:S(2)}) %collective-permute-start.9) | collective-permute-done | bytes 524320 | tf_op jit(solution)/shard_map/ppermute | solution.py:128
  58.3 5.2 %collective-permute-start.11 = (bf16[512,1024]{1,0:T(8,128)(2,1)S(1)}, bf16[512,1024]{1,0:T(8,128)(2,1)S(1)}, u32[]{:S(2)}, u32[]{:S(2)}) collective-permute-start(bf16[512,1024]{1,0:T(8,128)(2,1)S(1)} %pad_maximum_fusion), channel_id=1, source_target_pairs={{0,16},{1,17},{2,18},{3,19},{4,20},{5,21},{6,22},{7,23},{8,56},{9,... | collective-permute-start | bytes 3145736 | tf_op jit(solution)/shard_map/ppermute | solution.py:128
  63.5 1.9 collective-permute-start.12
  65.4 16.8 %collective-permute-done.11 = bf16[512,1024]{1,0:T(8,128)(2,1)S(1)} collective-permute-done((bf16[512,1024]{1,0:T(8,128)(2,1)S(1)}, bf16[512,1024]{1,0:T(8,128)(2,1)S(1)}, u32[]{:S(2)}, u32[]{:S(2)}) %collective-permute-start.11) | collective-permute-done | bytes 1048608 | tf_op jit(solution)/shard_map/ppermute | solution.py:128
  82.2 5.5 %collective-permute-done.12 = bf16[512,1024]{1,0:T(8,128)(2,1)S(1)} collective-permute-done((bf16[512,1024]{1,0:T(8,128)(2,1)S(1)}, bf16[512,1024]{1,0:T(8,128)(2,1)S(1)}, u32[]{:S(2)}, u32[]{:S(2)}) %collective-permute-start.12) | collective-permute-done | bytes 1048608 | tf_op jit(solution)/shard_map/ppermute | solution.py:128
  87.8 3.1 %collective-permute-start.16 = (bf16[512,1024]{1,0:T(8,128)(2,1)S(1)}, bf16[512,1024]{1,0:T(8,128)(2,1)S(1)}, u32[]{:S(2)}, u32[]{:S(2)}) collective-permute-start(bf16[512,1024]{1,0:T(8,128)(2,1)S(1)} %collective-permute-done.12), channel_id=1, source_target_pairs={{0,1},{1,64},{2,3},{3,66},{4,5},{5,68},{6,7},{7,70},{8,73},{9,8},{... | collective-permute-start | bytes 3145736 | tf_op jit(solution)/shard_map/ppermute | solution.py:128
  92.0 10.6 %collective-permute-done.16 = bf16[512,1024]{1,0:T(8,128)(2,1)S(1)} collective-permute-done((bf16[512,1024]{1,0:T(8,128)(2,1)S(1)}, bf16[512,1024]{1,0:T(8,128)(2,1)S(1)}, u32[]{:S(2)}, u32[]{:S(2)}) %collective-permute-start.16) | collective-permute-done | bytes 1048608 | tf_op jit(solution)/shard_map/ppermute | solution.py:128
  102.6 1.9 collective-permute-done.15
  106.7 3.3 %copy-done.14 = bf16[4096,1024]{1,0:T(8,128)(2,1)} copy-done((bf16[4096,1024]{1,0:T(8,128)(2,1)}, bf16[4096,1024]{1,0:T(8,128)(2,1)S(1)}, u32[]{:S(2)}) %copy-start.14) | copy-done | bytes 8388632
  110.0 11.2 %convolution_convert_fusion = bf16[1024,4096]{1,0:T(8,128)(2,1)} fusion(bf16[1024,1024]{1,0:T(8,128)(2,1)S(1)} %shard_map.69, bf16[4096,1024]{1,0:T(8,128)(2,1)S(1)} %select_dynamic-update-slice_fusion), kind=kOutput, calls=%fused_computation | convolution fusion | flops 8594128896 | bytes 18874368 | tf_op jit(solution)/shard_map/dot_general | solution.py:116
  121.2 2.7 %multiply_convert_fusion.6 = bf16[512,1024]{1,0:T(8,128)(2,1)S(1)} fusion(bf16[1024,1024]{1,0:T(8,128)(2,1)S(1)} %shard_map.69, bf16[1024,4096]{1,0:T(8,128)(2,1)} %all-gather.2.cloned.1.call-done), kind=kOutput, calls=%fused_computation.11 | convolution fusion | flops 1074790400 | bytes 4194304 | tf_op jit(solution)/shard_map/dot_general | solution.py:116
  124.0 2.5 %multiply_convert_fusion.4 = bf16[512,1024]{1,0:T(8,128)(2,1)S(1)} fusion(bf16[1024,1024]{1,0:T(8,128)(2,1)S(1)} %shard_map.69, bf16[1024,4096]{1,0:T(8,128)(2,1)} %all-gather.2.cloned.1.call-done, s32[]{:T(128)S(6)} %select_n.89), kind=kOutput, calls=%fused_computation.9 | convolution fusion | flops 1074790400 | bytes 4194308 | tf_op jit(solution)/shard_map/dot_general | solution.py:116
  126.5 2.7 %collective-permute-start.21 = (bf16[512,1024]{1,0:T(8,128)(2,1)S(1)}, bf16[512,1024]{1,0:T(8,128)(2,1)S(1)}, u32[]{:S(2)}, u32[]{:S(2)}) collective-permute-start(bf16[512,1024]{1,0:T(8,128)(2,1)S(1)} %multiply_convert_fusion.4), channel_id=1, source_target_pairs={{0,1},{1,64},{2,3},{3,66},{4,5},{5,68},{6,7},{7,70},{8,73},{9,8},{... | collective-permute-start | bytes 3145736 | tf_op jit(solution)/shard_map/ppermute | solution.py:128
  129.3 1.3 multiply_convert_fusion.7
  130.9 11.3 %convolution_convert_fusion.1 = bf16[1024,1024]{1,0:T(8,128)(2,1)S(1)} fusion(bf16[1024,4096]{1,0:T(8,128)(2,1)S(1)} %copy-done.8, bf16[4096,1024]{1,0:T(8,128)(2,1)} %copy-done.14), kind=kOutput, calls=%fused_computation.13 | convolution fusion | flops 8590983168 | bytes 18874368 | tf_op jit(solution)/shard_map/dot_general | solution.py:116
  142.1 1.3 multiply_convert_fusion.2
  143.4 1.3 multiply_convert_fusion.5
  144.7 2.7 %collective-permute-start.19 = (bf16[512,1024]{1,0:T(8,128)(2,1)S(1)}, bf16[512,1024]{1,0:T(8,128)(2,1)S(1)}, u32[]{:S(2)}, u32[]{:S(2)}) collective-permute-start(bf16[512,1024]{1,0:T(8,128)(2,1)S(1)} %multiply_convert_fusion.5), channel_id=1, source_target_pairs={{0,16},{1,17},{2,18},{3,19},{4,20},{5,21},{6,22},{7,23},{8,56},{9,... | collective-permute-start | bytes 3145736 | tf_op jit(solution)/shard_map/ppermute | solution.py:128
  149.2 1.3 multiply_convert_fusion.3
  151.1 1.3 multiply_convert_fusion.1
  152.5 5.2 %collective-permute-start.23 = (bf16[4,128,1024]{2,1,0:T(8,128)(2,1)S(1)}, bf16[4,128,1024]{2,1,0:T(8,128)(2,1)S(1)}, u32[]{:S(2)}, u32[]{:S(2)}) collective-permute-start(bf16[4,128,1024]{2,1,0:T(8,128)(2,1)S(1)} %get-tuple-element.215), channel_id=1, source_target_pairs={{0,8},{1,9},{2,10},{3,11},{4,12},{5,13},{6,14},{7,15},{8,0},{9,1},... | collective-permute-start | bytes 3145736 | tf_op jit(solution)/shard_map/ppermute | solution.py:128
  157.7 6.8 %collective-permute-done.22 = bf16[512,1024]{1,0:T(8,128)(2,1)S(1)} collective-permute-done((bf16[512,1024]{1,0:T(8,128)(2,1)S(1)}, bf16[512,1024]{1,0:T(8,128)(2,1)S(1)}, u32[]{:S(2)}, u32[]{:S(2)}) %collective-permute-start.22) | collective-permute-done | bytes 1048608 | tf_op jit(solution)/shard_map/ppermute | solution.py:128
  165.3 7.4 %collective-permute-done.20 = bf16[512,1024]{1,0:T(8,128)(2,1)S(1)} collective-permute-done((bf16[512,1024]{1,0:T(8,128)(2,1)S(1)}, bf16[512,1024]{1,0:T(8,128)(2,1)S(1)}, u32[]{:S(2)}, u32[]{:S(2)}) %collective-permute-start.20) | collective-permute-done | bytes 1048608 | tf_op jit(solution)/shard_map/ppermute | solution.py:128
  174.3 2.4 %collective-permute-start.31 = (bf16[128,1024]{1,0:T(8,128)(2,1)S(1)}, bf16[128,1024]{1,0:T(8,128)(2,1)S(1)}, u32[]{:S(2)}, u32[]{:S(2)}) collective-permute-start(bf16[128,1024]{1,0:T(8,128)(2,1)S(1)} %get-tuple-element.235), channel_id=1, source_target_pairs={{0,1},{1,64},{2,3},{3,66},{4,5},{5,68},{6,7},{7,70},{8,73},{9,8},{... | collective-permute-start | bytes 786440 | tf_op jit(solution)/shard_map/ppermute | solution.py:128
  178.4 4.8 %collective-permute-done.27 = bf16[128,1024]{1,0:T(8,128)(2,1)S(1)} collective-permute-done((bf16[128,1024]{1,0:T(8,128)(2,1)S(1)}, bf16[128,1024]{1,0:T(8,128)(2,1)S(1)}, u32[]{:S(2)}, u32[]{:S(2)}) %collective-permute-start.27) | collective-permute-done | bytes 262176 | tf_op jit(solution)/shard_map/ppermute | solution.py:128
  184.2 1.4 collective-permute-start.25
  185.7 1.7 collective-permute-start.26
  187.4 2.7 %collective-permute-done.28 = bf16[128,1024]{1,0:T(8,128)(2,1)S(1)} collective-permute-done((bf16[128,1024]{1,0:T(8,128)(2,1)S(1)}, bf16[128,1024]{1,0:T(8,128)(2,1)S(1)}, u32[]{:S(2)}, u32[]{:S(2)}) %collective-permute-start.28) | collective-permute-done | bytes 262176 | tf_op jit(solution)/shard_map/ppermute | solution.py:128
  190.4 1.9 collective-permute-start.33
  192.4 2.6 %collective-permute-done.24.ahead = bf16[2,128,1024]{2,1,0:T(8,128)(2,1)S(1)} collective-permute-done((bf16[2,128,1024]{2,1,0:T(8,128)(2,1)S(1)}, bf16[2,128,1024]{2,1,0:T(8,128)(2,1)S(1)}, u32[]{:S(2)}, u32[]{:S(2)}) %collective-permute-start.24) | collective-permute-done | bytes 524320 | tf_op jit(solution)/shard_map/ppermute | solution.py:128
  194.9 3.9 %collective-permute-done.25.back = bf16[2,128,1024]{2,1,0:T(8,128)(2,1)S(1)} collective-permute-done((bf16[2,128,1024]{2,1,0:T(8,128)(2,1)S(1)}, bf16[2,128,1024]{2,1,0:T(8,128)(2,1)S(1)}, u32[]{:S(2)}, u32[]{:S(2)}) %collective-permute-start.25) | collective-permute-done | bytes 524320 | tf_op jit(solution)/shard_map/ppermute | solution.py:128
  198.8 10.0 %collective-permute-done.26.across = bf16[2,128,1024]{2,1,0:T(8,128)(2,1)S(1)} collective-permute-done((bf16[2,128,1024]{2,1,0:T(8,128)(2,1)S(1)}, bf16[2,128,1024]{2,1,0:T(8,128)(2,1)S(1)}, u32[]{:S(2)}, u32[]{:S(2)}) %collective-permute-start.26) | collective-permute-done | bytes 524320 | tf_op jit(solution)/shard_map/ppermute | solution.py:128
  208.9 2.3 %shard_map.71 = bf16[128,8192]{1,0:T(8,128)(2,1)} custom-call(s32[4]{0:T(128)S(1)} %pad_add_fusion.place, bf16[128,8192]{1,0:T(8,128)(2,1)S(1)} %copy-done, bf16[2,128,1024]{2,1,0:T(8,128)(2,1)S(1)} %get-tuple-element.217.here, bf16[2,128,1024]{2,1,0:T(8,128)(2,1)S(1)} %collective-permute-done.24.ahead, ...), custom_call_target="tpu_custom_call" | custom-call | tf_op jit(solution)/shard_map/pallas_call | solution.py:106
  212.4 1.8 shard_map.72
  (109 shorter events, 18.6 us)
Async XLA Ops:
  7.2 8.0 %copy-start.1 = (bf16[128,8192]{1,0:T(8,128)(2,1)S(1)}, bf16[128,8192]{1,0:T(8,128)(2,1)}, u32[]{:S(2)}) copy-start(bf16[128,8192]{1,0:T(8,128)(2,1)} %cotangent.1) | copy-start | bytes 6291460
  7.2 114.1 %all-gather.2.cloned.1.call-start = ((), (), s32[]{:S(2)}) async-start(), calls=%async_computation.1 | async-start | bytes 9437184 | tf_op jit(solution)/shard_map/all_gather | solution.py:149
  10.5 200.7 %reduce-scatter.2.cloned.1.call-start = ((), (), s32[]{:S(2)}) async-start(), calls=%async_computation.2 | async-start | bytes 9437184 | tf_op jit(solution)/shard_map/reduce_scatter | solution.py:207
  10.6 11.7 %collective-permute-start = (bf16[256,1024]{1,0:T(8,128)(2,1)S(1)}, bf16[256,1024]{1,0:T(8,128)(2,1)S(1)}, u32[]{:S(2)}, u32[]{:S(2)}) collective-permute-start(bf16[256,1024]{1,0:T(8,128)(2,1)S(1)} %copy-done.15), channel_id=1, source_target_pairs={{0,0},{1,8},{2,2},{3,10},{4,4},{5,12},{6,6},{7,14},{8,1},{9,9},{10... | collective-permute-start | bytes 1572872 | tf_op jit(solution)/shard_map/ppermute | solution.py:128
  16.8 20.4 %collective-permute-start.3 = (bf16[2,128,1024]{2,1,0:T(8,128)(2,1)S(1)}, bf16[2,128,1024]{2,1,0:T(8,128)(2,1)S(1)}, u32[]{:S(2)}, u32[]{:S(2)}) collective-permute-start(bf16[2,128,1024]{2,1,0:T(8,128)(2,1)S(1)} %get-tuple-element.134), channel_id=1, source_target_pairs={{0,2},{1,3},{2,4},{3,5},{4,6},{5,7},{6,0},{7,1},{8,14},{9,15},{10,... | collective-permute-start | bytes 1572872 | tf_op jit(solution)/shard_map/ppermute | solution.py:128
  19.3 19.4 %collective-permute-start.4 = (bf16[2,128,1024]{2,1,0:T(8,128)(2,1)}, bf16[2,128,1024]{2,1,0:T(8,128)(2,1)S(1)}, u32[]{:S(2)}, u32[]{:S(2)}) collective-permute-start(bf16[2,128,1024]{2,1,0:T(8,128)(2,1)} %get-tuple-element.138), channel_id=1, source_target_pairs={{0,6},{1,7},{2,0},{3,1},{4,2},{5,3},{6,4},{7,5},{8,10},{9,11},{10,... | collective-permute-start | bytes 1572872 | tf_op jit(solution)/shard_map/ppermute | solution.py:128
  22.3 15.0 %copy-start.9 = (bf16[256,1024]{1,0:T(8,128)(2,1)}, bf16[256,1024]{1,0:T(8,128)(2,1)S(1)}, u32[]{:S(2)}) copy-start(bf16[256,1024]{1,0:T(8,128)(2,1)S(1)} %collective-permute-done) | copy-start | bytes 1572868
  23.2 6.5 %collective-permute-start.1 = (bf16[128,1024]{1,0:T(8,128)(2,1)S(1)}, bf16[128,1024]{1,0:T(8,128)(2,1)S(1)}, u32[]{:S(2)}, u32[]{:S(2)}) collective-permute-start(bf16[128,1024]{1,0:T(8,128)(2,1)S(1)} %get-tuple-element.142), channel_id=1, source_target_pairs={{0,1},{1,64},{2,3},{3,66},{4,5},{5,68},{6,7},{7,70},{8,73},{9,8},{... | collective-permute-start | bytes 786440 | tf_op jit(solution)/shard_map/ppermute | solution.py:128
  23.2 7.1 %collective-permute-start.2 = (bf16[128,1024]{1,0:T(8,128)(2,1)S(1)}, bf16[128,1024]{1,0:T(8,128)(2,1)S(1)}, u32[]{:S(2)}, u32[]{:S(2)}) collective-permute-start(bf16[128,1024]{1,0:T(8,128)(2,1)S(1)} %get-tuple-element.148), channel_id=1, source_target_pairs={{0,16},{1,17},{2,18},{3,19},{4,20},{5,21},{6,22},{7,23},{8,56},{9,... | collective-permute-start | bytes 786440 | tf_op jit(solution)/shard_map/ppermute | solution.py:128
  26.9 31.1 %collective-permute-start.9 = (bf16[2,128,1024]{2,1,0:T(8,128)(2,1)}, bf16[2,128,1024]{2,1,0:T(8,128)(2,1)S(1)}, u32[]{:S(2)}, u32[]{:S(2)}) collective-permute-start(bf16[2,128,1024]{2,1,0:T(8,128)(2,1)} %get-tuple-element.156), channel_id=1, source_target_pairs={{0,4},{1,5},{2,6},{3,7},{4,0},{5,1},{6,2},{7,3},{8,12},{9,13},{10,... | collective-permute-start | bytes 1572872 | tf_op jit(solution)/shard_map/ppermute | solution.py:128
  30.3 8.5 %copy-start.11 = (bf16[128,1024]{1,0:T(8,128)(2,1)}, bf16[128,1024]{1,0:T(8,128)(2,1)S(1)}, u32[]{:S(2)}) copy-start(bf16[128,1024]{1,0:T(8,128)(2,1)S(1)} %collective-permute-done.2) | copy-start | bytes 786436
  37.3 11.8 %copy-start.2 = (bf16[2,128,1024]{2,1,0:T(8,128)(2,1)}, bf16[2,128,1024]{2,1,0:T(8,128)(2,1)S(1)}, u32[]{:S(2)}) copy-start(bf16[2,128,1024]{2,1,0:T(8,128)(2,1)S(1)} %collective-permute-done.3.ahead) | copy-start | bytes 1572868
  37.3 7.9 %collective-permute-start.6 = (bf16[128,1024]{1,0:T(8,128)(2,1)S(1)}, bf16[128,1024]{1,0:T(8,128)(2,1)}, u32[]{:S(2)}, u32[]{:S(2)}) collective-permute-start(bf16[128,1024]{1,0:T(8,128)(2,1)S(1)} %collective-permute-done.1), channel_id=1, source_target_pairs={{0,1},{1,64},{2,3},{3,66},{4,5},{5,68},{6,7},{7,70},{8,73},{9,8},{... | collective-permute-start | bytes 786440 | tf_op jit(solution)/shard_map/ppermute | solution.py:128
  37.3 8.4 %collective-permute-start.5 = (bf16[128,1024]{1,0:T(8,128)(2,1)S(1)}, bf16[128,1024]{1,0:T(8,128)(2,1)S(1)}, u32[]{:S(2)}, u32[]{:S(2)}) collective-permute-start(bf16[128,1024]{1,0:T(8,128)(2,1)S(1)} %get-tuple-element.142), channel_id=1, source_target_pairs={{0,65},{1,0},{2,67},{3,2},{4,69},{5,4},{6,71},{7,6},{8,9},{9,72},{... | collective-permute-start | bytes 786440 | tf_op jit(solution)/shard_map/ppermute | solution.py:128
  38.8 11.3 %copy-start.4 = (bf16[2,128,1024]{2,1,0:T(8,128)(2,1)}, bf16[2,128,1024]{2,1,0:T(8,128)(2,1)S(1)}, u32[]{:S(2)}) copy-start(bf16[2,128,1024]{2,1,0:T(8,128)(2,1)S(1)} %collective-permute-done.4.back) | copy-start | bytes 1572868
  38.8 11.3 %collective-permute-start.8 = (bf16[128,1024]{1,0:T(8,128)(2,1)}, bf16[128,1024]{1,0:T(8,128)(2,1)S(1)}, u32[]{:S(2)}, u32[]{:S(2)}) collective-permute-start(bf16[128,1024]{1,0:T(8,128)(2,1)} %copy-done.11), channel_id=1, source_target_pairs={{0,16},{1,17},{2,18},{3,19},{4,20},{5,21},{6,22},{7,23},{8,56},{9,... | collective-permute-start | bytes 786440 | tf_op jit(solution)/shard_map/ppermute | solution.py:128
  43.4 8.7 %collective-permute-start.7 = (bf16[128,1024]{1,0:T(8,128)(2,1)S(1)}, bf16[128,1024]{1,0:T(8,128)(2,1)S(1)}, u32[]{:S(2)}, u32[]{:S(2)}) collective-permute-start(bf16[128,1024]{1,0:T(8,128)(2,1)S(1)} %get-tuple-element.148), channel_id=1, source_target_pairs={{0,48},{1,49},{2,50},{3,51},{4,52},{5,53},{6,54},{7,55},{8,24},{9,... | collective-permute-start | bytes 786440 | tf_op jit(solution)/shard_map/ppermute | solution.py:128
  46.5 5.5 %copy-start.12 = (bf16[128,1024]{1,0:T(8,128)(2,1)S(1)}, bf16[128,1024]{1,0:T(8,128)(2,1)}, u32[]{:S(2)}) copy-start(bf16[128,1024]{1,0:T(8,128)(2,1)} %copy-done.11) | copy-start | bytes 786436
  52.1 38.8 %copy-start.3 = (bf16[2,128,1024]{2,1,0:T(8,128)(2,1)S(1)}, bf16[2,128,1024]{2,1,0:T(8,128)(2,1)}, u32[]{:S(2)}) copy-start(bf16[2,128,1024]{2,1,0:T(8,128)(2,1)} %copy-done.2) | copy-start | bytes 1572868
  52.1 38.8 %copy-start.5 = (bf16[2,128,1024]{2,1,0:T(8,128)(2,1)S(1)}, bf16[2,128,1024]{2,1,0:T(8,128)(2,1)}, u32[]{:S(2)}) copy-start(bf16[2,128,1024]{2,1,0:T(8,128)(2,1)} %copy-done.4) | copy-start | bytes 1572868
  52.1 39.5 %copy-start.13 = (bf16[4096,1024]{1,0:T(8,128)(2,1)S(1)}, bf16[4096,1024]{1,0:T(8,128)(2,1)}, u32[]{:S(2)}) copy-start(bf16[4096,1024]{1,0:T(8,128)(2,1)} %get-tuple-element.229) | copy-start | bytes 25165828
  58.2 7.2 %collective-permute-start.10 = (bf16[512,1024]{1,0:T(8,128)(2,1)S(1)}, bf16[512,1024]{1,0:T(8,128)(2,1)S(1)}, u32[]{:S(2)}, u32[]{:S(2)}) collective-permute-start(bf16[512,1024]{1,0:T(8,128)(2,1)S(1)} %pad_maximum_fusion.2), channel_id=1, source_target_pairs={{0,8},{1,9},{2,10},{3,11},{4,12},{5,13},{6,14},{7,15},{8,0},{9,1},... | collective-permute-start | bytes 3145736 | tf_op jit(solution)/shard_map/ppermute | solution.py:128
  58.3 24.0 %collective-permute-start.11 = (bf16[512,1024]{1,0:T(8,128)(2,1)S(1)}, bf16[512,1024]{1,0:T(8,128)(2,1)S(1)}, u32[]{:S(2)}, u32[]{:S(2)}) collective-permute-start(bf16[512,1024]{1,0:T(8,128)(2,1)S(1)} %pad_maximum_fusion), channel_id=1, source_target_pairs={{0,16},{1,17},{2,18},{3,19},{4,20},{5,21},{6,22},{7,23},{8,56},{9,... | collective-permute-start | bytes 3145736 | tf_op jit(solution)/shard_map/ppermute | solution.py:128
  63.5 24.3 %collective-permute-start.12 = (bf16[512,1024]{1,0:T(8,128)(2,1)S(1)}, bf16[512,1024]{1,0:T(8,128)(2,1)S(1)}, u32[]{:S(2)}, u32[]{:S(2)}) collective-permute-start(bf16[512,1024]{1,0:T(8,128)(2,1)S(1)} %pad_maximum_fusion.1), channel_id=1, source_target_pairs={{0,1},{1,64},{2,3},{3,66},{4,5},{5,68},{6,7},{7,70},{8,73},{9,8},{... | collective-permute-start | bytes 3145736 | tf_op jit(solution)/shard_map/ppermute | solution.py:128
  65.4 26.2 %collective-permute-start.14 = (bf16[512,1024]{1,0:T(8,128)(2,1)S(1)}, bf16[512,1024]{1,0:T(8,128)(2,1)S(1)}, u32[]{:S(2)}, u32[]{:S(2)}) collective-permute-start(bf16[512,1024]{1,0:T(8,128)(2,1)S(1)} %pad_maximum_fusion.1), channel_id=1, source_target_pairs={{0,65},{1,0},{2,67},{3,2},{4,69},{5,4},{6,71},{7,6},{8,9},{9,72},{... | collective-permute-start | bytes 3145736 | tf_op jit(solution)/shard_map/ppermute | solution.py:128
  65.4 26.2 %collective-permute-start.13 = (bf16[512,1024]{1,0:T(8,128)(2,1)S(1)}, bf16[512,1024]{1,0:T(8,128)(2,1)S(1)}, u32[]{:S(2)}, u32[]{:S(2)}) collective-permute-start(bf16[512,1024]{1,0:T(8,128)(2,1)S(1)} %pad_maximum_fusion), channel_id=1, source_target_pairs={{0,48},{1,49},{2,50},{3,51},{4,52},{5,53},{6,54},{7,55},{8,24},{9,... | collective-permute-start | bytes 3145736 | tf_op jit(solution)/shard_map/ppermute | solution.py:128
  87.8 14.9 %collective-permute-start.16 = (bf16[512,1024]{1,0:T(8,128)(2,1)S(1)}, bf16[512,1024]{1,0:T(8,128)(2,1)S(1)}, u32[]{:S(2)}, u32[]{:S(2)}) collective-permute-start(bf16[512,1024]{1,0:T(8,128)(2,1)S(1)} %collective-permute-done.12), channel_id=1, source_target_pairs={{0,1},{1,64},{2,3},{3,66},{4,5},{5,68},{6,7},{7,70},{8,73},{9,8},{... | collective-permute-start | bytes 3145736 | tf_op jit(solution)/shard_map/ppermute | solution.py:128
  90.9 13.7 %collective-permute-start.15 = (bf16[512,1024]{1,0:T(8,128)(2,1)S(1)}, bf16[512,1024]{1,0:T(8,128)(2,1)S(1)}, u32[]{:S(2)}, u32[]{:S(2)}) collective-permute-start(bf16[512,1024]{1,0:T(8,128)(2,1)S(1)} %collective-permute-done.11), channel_id=1, source_target_pairs={{0,16},{1,17},{2,18},{3,19},{4,20},{5,21},{6,22},{7,23},{8,56},{9,... | collective-permute-start | bytes 3145736 | tf_op jit(solution)/shard_map/ppermute | solution.py:128
  106.7 3.3 %copy-start.14 = (bf16[4096,1024]{1,0:T(8,128)(2,1)}, bf16[4096,1024]{1,0:T(8,128)(2,1)S(1)}, u32[]{:S(2)}) copy-start(bf16[4096,1024]{1,0:T(8,128)(2,1)S(1)} %select_dynamic-update-slice_fusion) | copy-start | bytes 25165828
  121.2 8.0 %copy-start.8 = (bf16[1024,4096]{1,0:T(8,128)(2,1)S(1)}, bf16[1024,4096]{1,0:T(8,128)(2,1)}, u32[]{:S(2)}) copy-start(bf16[1024,4096]{1,0:T(8,128)(2,1)} %all-gather.2.cloned.1.call-done) | copy-start | bytes 25165828
  123.9 24.8 %collective-permute-start.18 = (bf16[512,1024]{1,0:T(8,128)(2,1)S(1)}, bf16[512,1024]{1,0:T(8,128)(2,1)S(1)}, u32[]{:S(2)}, u32[]{:S(2)}) collective-permute-start(bf16[512,1024]{1,0:T(8,128)(2,1)S(1)} %multiply_convert_fusion.6), channel_id=1, source_target_pairs={{0,65},{1,0},{2,67},{3,2},{4,69},{5,4},{6,71},{7,6},{8,9},{9,72},{... | collective-permute-start | bytes 3145736 | tf_op jit(solution)/shard_map/ppermute | solution.py:128
  126.5 31.2 %collective-permute-start.21 = (bf16[512,1024]{1,0:T(8,128)(2,1)S(1)}, bf16[512,1024]{1,0:T(8,128)(2,1)S(1)}, u32[]{:S(2)}, u32[]{:S(2)}) collective-permute-start(bf16[512,1024]{1,0:T(8,128)(2,1)S(1)} %multiply_convert_fusion.4), channel_id=1, source_target_pairs={{0,1},{1,64},{2,3},{3,66},{4,5},{5,68},{6,7},{7,70},{8,73},{9,8},{... | collective-permute-start | bytes 3145736 | tf_op jit(solution)/shard_map/ppermute | solution.py:128
  130.6 20.0 %collective-permute-start.17 = (bf16[512,1024]{1,0:T(8,128)(2,1)S(1)}, bf16[512,1024]{1,0:T(8,128)(2,1)S(1)}, u32[]{:S(2)}, u32[]{:S(2)}) collective-permute-start(bf16[512,1024]{1,0:T(8,128)(2,1)S(1)} %multiply_convert_fusion.7), channel_id=1, source_target_pairs={{0,48},{1,49},{2,50},{3,51},{4,52},{5,53},{6,54},{7,55},{8,24},{9,... | collective-permute-start | bytes 3145736 | tf_op jit(solution)/shard_map/ppermute | solution.py:128
  144.7 20.5 %collective-permute-start.19 = (bf16[512,1024]{1,0:T(8,128)(2,1)S(1)}, bf16[512,1024]{1,0:T(8,128)(2,1)S(1)}, u32[]{:S(2)}, u32[]{:S(2)}) collective-permute-start(bf16[512,1024]{1,0:T(8,128)(2,1)S(1)} %multiply_convert_fusion.5), channel_id=1, source_target_pairs={{0,16},{1,17},{2,18},{3,19},{4,20},{5,21},{6,22},{7,23},{8,56},{9,... | collective-permute-start | bytes 3145736 | tf_op jit(solution)/shard_map/ppermute | solution.py:128
  149.2 15.3 %collective-permute-start.22 = (bf16[512,1024]{1,0:T(8,128)(2,1)S(1)}, bf16[512,1024]{1,0:T(8,128)(2,1)S(1)}, u32[]{:S(2)}, u32[]{:S(2)}) collective-permute-start(bf16[512,1024]{1,0:T(8,128)(2,1)S(1)} %add_convert_fusion.2), channel_id=1, source_target_pairs={{0,65},{1,0},{2,67},{3,2},{4,69},{5,4},{6,71},{7,6},{8,9},{9,72},{... | collective-permute-start | bytes 3145736 | tf_op jit(solution)/shard_map/ppermute | solution.py:128
  151.0 21.7 %collective-permute-start.20 = (bf16[512,1024]{1,0:T(8,128)(2,1)S(1)}, bf16[512,1024]{1,0:T(8,128)(2,1)S(1)}, u32[]{:S(2)}, u32[]{:S(2)}) collective-permute-start(bf16[512,1024]{1,0:T(8,128)(2,1)S(1)} %add_convert_fusion.3), channel_id=1, source_target_pairs={{0,48},{1,49},{2,50},{3,51},{4,52},{5,53},{6,54},{7,55},{8,24},{9,... | collective-permute-start | bytes 3145736 | tf_op jit(solution)/shard_map/ppermute | solution.py:128
  152.5 30.9 %collective-permute-start.23 = (bf16[4,128,1024]{2,1,0:T(8,128)(2,1)S(1)}, bf16[4,128,1024]{2,1,0:T(8,128)(2,1)S(1)}, u32[]{:S(2)}, u32[]{:S(2)}) collective-permute-start(bf16[4,128,1024]{2,1,0:T(8,128)(2,1)S(1)} %get-tuple-element.215), channel_id=1, source_target_pairs={{0,8},{1,9},{2,10},{3,11},{4,12},{5,13},{6,14},{7,15},{8,0},{9,1},... | collective-permute-start | bytes 3145736 | tf_op jit(solution)/shard_map/ppermute | solution.py:128
  165.2 12.4 %collective-permute-start.29 = (bf16[128,1024]{1,0:T(8,128)(2,1)S(1)}, bf16[128,1024]{1,0:T(8,128)(2,1)S(1)}, u32[]{:S(2)}, u32[]{:S(2)}) collective-permute-start(bf16[128,1024]{1,0:T(8,128)(2,1)S(1)} %get-tuple-element.226), channel_id=1, source_target_pairs={{0,48},{1,49},{2,50},{3,51},{4,52},{5,53},{6,54},{7,55},{8,24},{9,... | collective-permute-start | bytes 786440 | tf_op jit(solution)/shard_map/ppermute | solution.py:128
  173.4 9.8 %collective-permute-start.27 = (bf16[128,1024]{1,0:T(8,128)(2,1)S(1)}, bf16[128,1024]{1,0:T(8,128)(2,1)S(1)}, u32[]{:S(2)}, u32[]{:S(2)}) collective-permute-start(bf16[128,1024]{1,0:T(8,128)(2,1)S(1)} %get-tuple-element.225), channel_id=1, source_target_pairs={{0,65},{1,0},{2,67},{3,2},{4,69},{5,4},{6,71},{7,6},{8,9},{9,72},{... | collective-permute-start | bytes 786440 | tf_op jit(solution)/shard_map/ppermute | solution.py:128
  174.3 9.9 %collective-permute-start.31 = (bf16[128,1024]{1,0:T(8,128)(2,1)S(1)}, bf16[128,1024]{1,0:T(8,128)(2,1)S(1)}, u32[]{:S(2)}, u32[]{:S(2)}) collective-permute-start(bf16[128,1024]{1,0:T(8,128)(2,1)S(1)} %get-tuple-element.235), channel_id=1, source_target_pairs={{0,1},{1,64},{2,3},{3,66},{4,5},{5,68},{6,7},{7,70},{8,73},{9,8},{... | collective-permute-start | bytes 786440 | tf_op jit(solution)/shard_map/ppermute | solution.py:128
  176.7 9.0 %collective-permute-start.32 = (bf16[128,1024]{1,0:T(8,128)(2,1)S(1)}, bf16[128,1024]{1,0:T(8,128)(2,1)S(1)}, u32[]{:S(2)}, u32[]{:S(2)}) collective-permute-start(bf16[128,1024]{1,0:T(8,128)(2,1)S(1)} %get-tuple-element.238), channel_id=1, source_target_pairs={{0,16},{1,17},{2,18},{3,19},{4,20},{5,21},{6,22},{7,23},{8,56},{9,... | collective-permute-start | bytes 786440 | tf_op jit(solution)/shard_map/ppermute | solution.py:128
  177.8 9.6 %collective-permute-start.30 = (bf16[128,1024]{1,0:T(8,128)(2,1)S(1)}, bf16[128,1024]{1,0:T(8,128)(2,1)S(1)}, u32[]{:S(2)}, u32[]{:S(2)}) collective-permute-start(bf16[128,1024]{1,0:T(8,128)(2,1)S(1)} %add_convert_fusion.6), channel_id=1, source_target_pairs={{0,48},{1,49},{2,50},{3,51},{4,52},{5,53},{6,54},{7,55},{8,24},{9,... | collective-permute-start | bytes 786440 | tf_op jit(solution)/shard_map/ppermute | solution.py:128
  183.3 6.8 %collective-permute-start.28 = (bf16[128,1024]{1,0:T(8,128)(2,1)S(1)}, bf16[128,1024]{1,0:T(8,128)(2,1)S(1)}, u32[]{:S(2)}, u32[]{:S(2)}) collective-permute-start(bf16[128,1024]{1,0:T(8,128)(2,1)S(1)} %add_convert_fusion.7), channel_id=1, source_target_pairs={{0,65},{1,0},{2,67},{3,2},{4,69},{5,4},{6,71},{7,6},{8,9},{9,72},{... | collective-permute-start | bytes 786440 | tf_op jit(solution)/shard_map/ppermute | solution.py:128
  184.1 24.7 %copy-start = (bf16[128,8192]{1,0:T(8,128)(2,1)S(1)}, bf16[128,8192]{1,0:T(8,128)(2,1)}, u32[]{:S(2)}) copy-start(bf16[128,8192]{1,0:T(8,128)(2,1)} %residual.1) | copy-start | bytes 6291460
  184.1 10.8 %collective-permute-start.24 = (bf16[2,128,1024]{2,1,0:T(8,128)(2,1)S(1)}, bf16[2,128,1024]{2,1,0:T(8,128)(2,1)S(1)}, u32[]{:S(2)}, u32[]{:S(2)}) collective-permute-start(bf16[2,128,1024]{2,1,0:T(8,128)(2,1)S(1)} %get-tuple-element.218), channel_id=1, source_target_pairs={{0,2},{1,3},{2,4},{3,5},{4,6},{5,7},{6,0},{7,1},{8,14},{9,15},{10,... | collective-permute-start | bytes 1572872 | tf_op jit(solution)/shard_map/ppermute | solution.py:128
  184.2 14.6 %collective-permute-start.25 = (bf16[2,128,1024]{2,1,0:T(8,128)(2,1)S(1)}, bf16[2,128,1024]{2,1,0:T(8,128)(2,1)S(1)}, u32[]{:S(2)}, u32[]{:S(2)}) collective-permute-start(bf16[2,128,1024]{2,1,0:T(8,128)(2,1)S(1)} %get-tuple-element.219), channel_id=1, source_target_pairs={{0,6},{1,7},{2,0},{3,1},{4,2},{5,3},{6,4},{7,5},{8,10},{9,11},{10,... | collective-permute-start | bytes 1572872 | tf_op jit(solution)/shard_map/ppermute | solution.py:128
  185.7 23.2 %collective-permute-start.26 = (bf16[2,128,1024]{2,1,0:T(8,128)(2,1)S(1)}, bf16[2,128,1024]{2,1,0:T(8,128)(2,1)S(1)}, u32[]{:S(2)}, u32[]{:S(2)}) collective-permute-start(bf16[2,128,1024]{2,1,0:T(8,128)(2,1)S(1)} %get-tuple-element.220), channel_id=1, source_target_pairs={{0,4},{1,5},{2,6},{3,7},{4,0},{5,1},{6,2},{7,3},{8,12},{9,13},{10,... | collective-permute-start | bytes 1572872 | tf_op jit(solution)/shard_map/ppermute | solution.py:128
  190.4 20.8 %collective-permute-start.33 = (bf16[256,1024]{1,0:T(8,128)(2,1)S(1)}, bf16[256,1024]{1,0:T(8,128)(2,1)S(1)}, u32[]{:S(2)}, u32[]{:S(2)}) collective-permute-start(bf16[256,1024]{1,0:T(8,128)(2,1)S(1)} %pad_maximum_fusion.3), channel_id=1, source_target_pairs={{0,0},{1,8},{2,2},{3,10},{4,4},{5,12},{6,6},{7,14},{8,1},{9,9},{10... | collective-permute-start | bytes 1572872 | tf_op jit(solution)/shard_map/ppermute | solution.py:128
  (4 other events, 5.5 us)
Sparse Core Ops, SparseCore 0:
  10.6 66.6 all-gather.1
  121.3 50.4 reduce-scatter.1

commit v3 on v2

--- a/solution.py
+++ b/solution.py
@@ -28,11 +28,13 @@
 
 X_AHEAD = moves(lambda x, y, z, c: ((x + 1 + 2 * c) % 4, y, z, c))
 X_BACK = moves(lambda x, y, z, c: ((x + 3 + 2 * c) % 4, y, z, c))
+X_ACROSS = moves(lambda x, y, z, c: ((x + 2) % 4, y, z, c))
 Y_AHEAD = moves(lambda x, y, z, c: (x, (y + 1 + 2 * c) % 4, z, c))
 Y_BACK = moves(lambda x, y, z, c: (x, (y + 3 + 2 * c) % 4, z, c))
 Z_AHEAD = moves(lambda x, y, z, c: (x, y, (z + 1 + 2 * c) % 4, c))
 Z_BACK = moves(lambda x, y, z, c: (x, y, (z + 3 + 2 * c) % 4, c))
-X_ACROSS = moves(lambda x, y, z, c: ((x + 2) % 4, y, z, c))
+Y_ACROSS = moves(lambda x, y, z, c: (x, (y + 2) % 4, z, c))
+Z_ACROSS = moves(lambda x, y, z, c: (x, y, (z + 2) % 4, c))
 CORE = moves(lambda x, y, z, c: (x, y, z, 1 - c))
 SWAP = moves(lambda x, y, z, c: (x, y - y % 2 + c, z, y % 2))
 
@@ -81,26 +83,6 @@
         out[pl.ds(pl.multiple_of((at + 1 - c) * n, n), n), :] = given[e * n : (e + 1) * n, :]
 
 
-def outgoing_kernel(place, own, got, here, ahead, back, across):
-    x, c = place[0], place[3]
-    step = 1 + 2 * c
-    for distance, out in ((0, here), (step, ahead), (4 - step, back), (2, across)):
-        out[0] = own[(x + distance) % 4]
-        out[1] = got[(x + distance) % 4]
-
-
-def layer_kernel(place, residual, here, ahead, back, across, out):
-    x, c = place[0], place[3]
-    step = 1 + 2 * c
-    pieces = []
-    for distance, both in ((0, here), (4 - step, ahead), (step, back), (2, across)):
-        pieces += [(x + distance, c, both.at[0]), (x + distance, 1 - c, both.at[1])]
-    for xx, cc, piece in pieces:
-        at = pl.multiple_of((xx % 4 * 2 + cc) * WIDE, WIDE)
-        total = residual[:, pl.ds(at, WIDE)].astype(F32) + piece[...].astype(F32)
-        out[:, pl.ds(at, WIDE)] = total.astype(BF16)
-
-
 def local(kernel, shapes, place, *operands):
     vmem = pl.BlockSpec(memory_space=pltpu.VMEM)
     return pl.pallas_call(
@@ -108,8 +90,20 @@
         out_shape=jax.tree.map(lambda s: jax.ShapeDtypeStruct(s, BF16), shapes, is_leaf=lambda s: isinstance(s[0], int)),
         in_specs=[pl.BlockSpec(memory_space=pltpu.SMEM)] + [vmem] * len(operands),
         out_specs=jax.tree.map(lambda s: vmem, shapes, is_leaf=lambda s: isinstance(s[0], int)),
-        compiler_params=pltpu.CompilerParams(vmem_limit_bytes=24 * 1024 * 1024),
+        compiler_params=pltpu.CompilerParams(vmem_limit_bytes=8 * 1024 * 1024),
     )(place, *operands)
+
+
+def after(value, *earlier):
+    anywhere = pl.BlockSpec(memory_space=pl.ANY)
+    return pl.pallas_call(
+        lambda *refs: None,
+        out_shape=jax.ShapeDtypeStruct(value.shape, value.dtype),
+        in_specs=[anywhere] * (1 + len(earlier)),
+        out_specs=anywhere,
+        input_output_aliases={0: 0},
+        compiler_params=pltpu.CompilerParams(vmem_limit_bytes=1024 * 1024),
+    )(value, *earlier)
 
 
 def dot(a, b, dims):
@@ -150,21 +144,19 @@
     pair = (2, n, WIDE)
     cot_here, ahead, back, across = local(columns_kernel, (pair, pair, pair, pair), place, cotangent)
     cot_ahead = send(ahead, X_AHEAD)
-    cot_back = send(back, X_BACK)
-    cot_across = send(across, X_ACROSS)
     mine = wait(mine)
     half = mine.shape[0] // 2
     up, lo = mine[:half], mine[half:]
     up_ahead = send(up, Y_AHEAD)
     lo_ahead = send(lo, Z_AHEAD)
+    up_back = send(up, Y_BACK)
+    lo_back = send(lo, Z_BACK)
     up_ahead = wait(up_ahead)
-    up_back = send(up, Y_BACK)
+    up_far = send(up, Y_ACROSS)
     lo_ahead = wait(lo_ahead)
-    lo_back = send(lo, Z_BACK)
+    lo_far = send(lo, Z_ACROSS)
     cot_ahead = wait(cot_ahead)
-    up_far = send(up_ahead, Y_AHEAD)
-    cot_back = wait(cot_back)
-    lo_far = send(lo_ahead, Z_AHEAD)
+    cot_back = send(back, X_BACK)
     up_back, up_far = wait(up_back, up_far)
     up = ring(up, up_ahead, up_far, up_back)
     up_ahead = send(up, Z_AHEAD)
@@ -173,17 +165,17 @@
     lo_ahead = send(lo, Y_AHEAD)
     up_back = send(up, Z_BACK)
     lo_back = send(lo, Y_BACK)
-    cot_across = wait(cot_across)
-    cot_given = send(jnp.concatenate([cot_here[1], cot_ahead[1], cot_across[1], cot_back[1]]), CORE)
-    cot_given = wait(cot_given)
-    cot = local(
-        tokens_kernel, (8 * n, WIDE), place, cot_here, cot_ahead, cot_back, cot_across, cot_given
-    )
+    cot_back = wait(cot_back)
+    cot_across = send(across, X_ACROSS)
     up_ahead = wait(up_ahead)
     up_far = send(up_ahead, Z_AHEAD)
     lo_ahead = wait(lo_ahead)
     lo_far = send(lo_ahead, Y_AHEAD)
+    cot_across = wait(cot_across)
+    cot_given = send(jnp.concatenate([cot_here[1], cot_ahead[1], cot_across[1], cot_back[1]]), CORE)
     up_back, lo_back = wait(up_back, lo_back)
+    cot_given = wait(cot_given)
+    cot = local(tokens_kernel, (8 * n, WIDE), place, cot_here, cot_ahead, cot_back, cot_across, cot_given)
 
     heads = wait(heads)
     factor = 1.0 / jnp.sqrt(jnp.float32(n * 128))
@@ -196,35 +188,32 @@
         return block[d * m : (d + 1) * m]
 
     one, three = jnp.where(first, 1, 3), jnp.where(first, 3, 1)
-    sum_up_far = send(weight(2), Z_BACK)
-    sum_lo_far = send(weight(6), Y_BACK)
+    weight_up, weight_lo = weight(2), weight(6)
+    sum_up_far = send(weight_up, Z_BACK)
+    sum_lo_far = send(weight_lo, Y_BACK)
+    started = [weight_up, weight_lo]
     up_far, lo_far = wait(up_far, lo_far)
-    sum_up_back = send(weight(three), Z_AHEAD)
-    sum_lo_back = send(weight(4 + three), Y_AHEAD)
+    started += [weight(three), weight(4 + three)]
+    sum_up_back = send(started[2], Z_AHEAD)
+    sum_lo_back = send(started[3], Y_AHEAD)
     proj = jnp.concatenate([ring(up, up_ahead, up_far, up_back), ring(lo, lo_ahead, lo_far, lo_back)])
     act = dot(cot, proj, ((1,), (1,))).astype(BF16)
     act = wait(act)
     grad_heads = lax.psum_scatter(act, ("x", "c"), scatter_dimension=0, tiled=True)
     weight_up, weight_lo = weight(one), weight(4 + one)
-    sum_up_far = wait(sum_up_far)
+
+    out = dot(heads, after(proj, act, *started), ((1,), (0,))).astype(BF16)
+    token_proj = lax.all_to_all(out, ("x", "c"), split_axis=0, concat_axis=1, tiled=True)
+    sum_up_far, sum_lo_far = after(sum_up_far, out), after(sum_lo_far, out)
     sum_up_ahead = send(add(weight_up, sum_up_far), Z_BACK)
-    sum_lo_far = wait(sum_lo_far)
     sum_lo_ahead = send(add(weight_lo, sum_lo_far), Y_BACK)
-    weight_up, weight_lo = wait(weight(0), weight(4))
-
-    out = wait(dot(heads, proj, ((1,), (0,))).astype(BF16)).reshape(4, 2, n, WIDE)
-    out_mine, out_given = [lax.dynamic_index_in_dim(out, e, 1, keepdims=False) for e in (c, 1 - c)]
-    out_given = send(out_given, CORE)
+    weight_up, weight_lo = weight(0), weight(4)
     sum_up_back, sum_up_ahead = wait(sum_up_back, sum_up_ahead)
     up = add(weight_up, sum_up_ahead, sum_up_back)
     sum_up_far = send(row(up, 2), Y_BACK)
     sum_lo_back, sum_lo_ahead = wait(sum_lo_back, sum_lo_ahead)
     lo = add(weight_lo, sum_lo_ahead, sum_lo_back)
     sum_lo_far = send(row(lo, 2), Z_BACK)
-    out_given = wait(out_given)
-    out_here, ahead, back, across = local(outgoing_kernel, (pair, pair, pair, pair), place, out_mine, out_given)
-    out_ahead = send(ahead, X_AHEAD)
-    out_back = send(back, X_BACK)
     up_one, up_three = pick(row(up, 1), row(up, 3))
     lo_one, lo_three = pick(row(lo, 1), row(lo, 3))
     sum_up_back = send(up_three, Y_AHEAD)
@@ -235,14 +224,12 @@
     sum_up_back = wait(sum_up_back)
     sum_lo_ahead = send(add(lo_one, sum_lo_far), Z_BACK)
     sum_lo_back = wait(sum_lo_back)
-    out_across = send(across, X_ACROSS)
     sum_up_ahead, sum_lo_ahead = wait(sum_up_ahead, sum_lo_ahead)
     grad_proj = jnp.concatenate(
         [add(row(up, 0), sum_up_ahead, sum_up_back), add(row(lo, 0), sum_lo_ahead, sum_lo_back)]
     )
     grad_proj = send(grad_proj, SWAP)
-    out_ahead, out_back, out_across = wait(out_ahead, out_back, out_across)
-    layer_out = local(layer_kernel, residual.shape, place, residual, out_here, out_ahead, out_back, out_across)
+    layer_out = add(residual, token_proj)
     grad_heads = local(restored_kernel, heads_out.shape, place, grad_heads)
     return (layer_out, grad_heads, grad_proj)
 

time: 223 us -> 214 us (0.960)
  waiting for transfers between devices: 93.7 us -> 63.5 us
  other arithmetic: 7.28 us -> 19.4 us
  starting transfers between devices: 51.4 us -> 57.7 us
  matrix products: 35.4 us -> 39.3 us
  Pallas kernels: 9.06 us -> 6.02 us
    ppermute x34 -> x30, waiting for transfers between devices: 93.7 us -> 62.7 us  [send(): return lax.ppermute(self.wait(value), AXES, pairs)]
    all_to_all x0 -> x1, starting transfers between devices: none -> 9.22 us  [per_device(): lax.all_to_all(out, ('x', 'c'), split_axis=0, concat_axis=1, tiled=True)]
    convert_element_type x8 -> x9, other arithmetic: 2.59 us -> 11.5 us  [add(): functools.reduce(lambda p, q: p + q, [t.astype(F32) for t in terms])]
    dot_general x10, matrix products: 35.4 us -> 39.3 us  [dot(): return lax.dot_general(a, b, (dims, ((), ())), preferred_element_type=F32)]
    pallas_call x6 -> x4, Pallas kernels: 9.06 us -> 6.01 us  [local(): pl.pallas_call(kernel, out_shape=jax.tree.map(lambda s: jax.ShapeDtypeStr...]
    ppermute x34 -> x30, starting transfers between devices: 51.3 us -> 48.4 us  [send(): return lax.ppermute(self.wait(value), AXES, pairs)]
    unnamed x40 -> x52, local copies, waits for them, and re-layouts: 9.29 us -> 11.4 us
    unnamed x5 -> x8, other arithmetic: 2.82 us -> 4.84 us
  transfers between devices with their start and end apart: 36 -> 33, of which waited for: 18 -> 15; matrix products, arithmetic and copies ran while one was open for 21% -> 29% of each run, Pallas kernels for 2% -> 1%
where the time goes in v3:
time: 214 us; the launch traced here: 213 us
  waiting for transfers between devices  63.5 us (30%)
  starting transfers between devices  57.7 us (27%)
  matrix products  39.3 us (18%)
  other arithmetic  19.4 us (9%)
  between operations  14.6 us (7%)
  local copies, waits for them, and re-layouts  12.6 us (6%)
  Pallas kernels  6.02 us (3%)
    ppermute x30, waiting for transfers between devices, send(): return lax.ppermute(self.wait(value), AXES, pairs)  62.7 us
    ppermute x30, starting transfers between devices, send(): return lax.ppermute(self.wait(value), AXES, pairs)  48.4 us
    dot_general x10, matrix products, dot(): return lax.dot_general(a, b, (dims, ((), ())), preferred_element_type=F32)  39.3 us
    convert_element_type x9, other arithmetic, add(): functools.reduce(lambda p, q: p + q, [t.astype(F32) for t in terms])  11.5 us
    unnamed x52, local copies, waits for them, and re-layouts  11.4 us
    all_to_all x1, starting transfers between devices, per_device(): lax.all_to_all(out, ('x', 'c'), split_axis=0, concat_axis=1, tiled=True)  9.22 us
    pallas_call x4, Pallas kernels, local(): pl.pallas_call(kernel, out_shape=jax.tree.map(lambda s: jax.ShapeDtypeStr...  6.01 us
    unnamed x8, other arithmetic  4.84 us
  transfers between devices with their start and end apart: 33, of which 15 were waited for; matrix products, arithmetic and copies ran while one was open for 29% of the time, Pallas kernels for 1%

profile of v3, /device:TPU:1, one launch (start us, length us, event | category | flops | bytes accessed | tf_op | source)
XLA Modules:
  0.0 213.2 jit_solution(12617396256138362195)
XLA Ops:
  7.3 1.3 copy-done.7
  8.7 1.8 shard_map.68
  10.5 4.6 %collective-permute-start = (bf16[256,1024]{1,0:T(8,128)(2,1)}, bf16[256,1024]{1,0:T(8,128)(2,1)S(1)}, u32[]{:S(2)}, u32[]{:S(2)}) collective-permute-start(bf16[256,1024]{1,0:T(8,128)(2,1)} %param.6), channel_id=1, source_target_pairs={{0,0},{1,8},{2,2},{3,10},{4,4},{5,12},{6,6},{7,14},{8,1},{9,9},{10... | collective-permute-start | bytes 1572872 | tf_op jit(solution)/shard_map/ppermute | solution.py:122
  15.2 1.7 shard_map.67
  17.6 2.5 %collective-permute-start.3 = (bf16[2,128,1024]{2,1,0:T(8,128)(2,1)}, bf16[2,128,1024]{2,1,0:T(8,128)(2,1)S(1)}, u32[]{:S(2)}, u32[]{:S(2)}) collective-permute-start(bf16[2,128,1024]{2,1,0:T(8,128)(2,1)} %get-tuple-element.106), channel_id=1, source_target_pairs={{0,2},{1,3},{2,4},{3,5},{4,6},{5,7},{6,0},{7,1},{8,14},{9,15},{10,... | collective-permute-start | bytes 1572872 | tf_op jit(solution)/shard_map/ppermute | solution.py:122
  20.1 2.4 %collective-permute-done = bf16[256,1024]{1,0:T(8,128)(2,1)S(1)} collective-permute-done((bf16[256,1024]{1,0:T(8,128)(2,1)}, bf16[256,1024]{1,0:T(8,128)(2,1)S(1)}, u32[]{:S(2)}, u32[]{:S(2)}) %collective-permute-start) | collective-permute-done | bytes 524320 | tf_op jit(solution)/shard_map/ppermute | solution.py:122
  23.4 3.8 %collective-permute-start.2 = (bf16[128,1024]{1,0:T(8,128)(2,1)S(1)}, bf16[128,1024]{1,0:T(8,128)(2,1)S(1)}, u32[]{:S(2)}, u32[]{:S(2)}) collective-permute-start(bf16[128,1024]{1,0:T(8,128)(2,1)S(1)} %get-tuple-element.118), channel_id=1, source_target_pairs={{0,16},{1,17},{2,18},{3,19},{4,20},{5,21},{6,22},{7,23},{8,56},{9,... | collective-permute-start | bytes 786440 | tf_op jit(solution)/shard_map/ppermute | solution.py:122
  27.1 1.5 collective-permute-start.4
  29.0 2.8 %collective-permute-start.5 = (bf16[128,1024]{1,0:T(8,128)(2,1)S(1)}, bf16[128,1024]{1,0:T(8,128)(2,1)S(1)}, u32[]{:S(2)}, u32[]{:S(2)}) collective-permute-start(bf16[128,1024]{1,0:T(8,128)(2,1)S(1)} %get-tuple-element.111), channel_id=1, source_target_pairs={{0,64},{1,65},{2,66},{3,67},{4,68},{5,69},{6,70},{7,71},{8,72},{9,... | collective-permute-start | bytes 786440 | tf_op jit(solution)/shard_map/ppermute | solution.py:122
  31.8 2.7 %collective-permute-start.11 = (bf16[2,128,1024]{2,1,0:T(8,128)(2,1)}, bf16[2,128,1024]{2,1,0:T(8,128)(2,1)S(1)}, u32[]{:S(2)}, u32[]{:S(2)}) collective-permute-start(bf16[2,128,1024]{2,1,0:T(8,128)(2,1)} %get-tuple-element.134), channel_id=1, source_target_pairs={{0,4},{1,5},{2,6},{3,7},{4,0},{5,1},{6,2},{7,3},{8,12},{9,13},{10,... | collective-permute-start | bytes 1572872 | tf_op jit(solution)/shard_map/ppermute | solution.py:122
  34.5 1.6 collective-permute-start.6
  36.2 3.9 %collective-permute-start.7 = (bf16[128,1024]{1,0:T(8,128)(2,1)S(1)}, bf16[128,1024]{1,0:T(8,128)(2,1)S(1)}, u32[]{:S(2)}, u32[]{:S(2)}) collective-permute-start(bf16[128,1024]{1,0:T(8,128)(2,1)S(1)} %get-tuple-element.118), channel_id=1, source_target_pairs={{0,32},{1,33},{2,34},{3,35},{4,36},{5,37},{6,38},{7,39},{8,40},{9,... | collective-permute-start | bytes 786440 | tf_op jit(solution)/shard_map/ppermute | solution.py:122
  43.1 1.3 pad_maximum_fusion
  44.4 2.9 %collective-permute-done.7 = bf16[128,1024]{1,0:T(8,128)(2,1)S(1)} collective-permute-done((bf16[128,1024]{1,0:T(8,128)(2,1)S(1)}, bf16[128,1024]{1,0:T(8,128)(2,1)S(1)}, u32[]{:S(2)}, u32[]{:S(2)}) %collective-permute-start.7) | collective-permute-done | bytes 262176 | tf_op jit(solution)/shard_map/ppermute | solution.py:122
  50.4 8.1 %collective-permute-done.11.across = bf16[2,128,1024]{2,1,0:T(8,128)(2,1)S(1)} collective-permute-done((bf16[2,128,1024]{2,1,0:T(8,128)(2,1)}, bf16[2,128,1024]{2,1,0:T(8,128)(2,1)S(1)}, u32[]{:S(2)}, u32[]{:S(2)}) %collective-permute-start.11) | collective-permute-done | bytes 524320 | tf_op jit(solution)/shard_map/ppermute | solution.py:122
  59.3 15.3 %collective-permute-done.8.back = bf16[2,128,1024]{2,1,0:T(8,128)(2,1)S(1)} collective-permute-done((bf16[2,128,1024]{2,1,0:T(8,128)(2,1)S(1)}, bf16[2,128,1024]{2,1,0:T(8,128)(2,1)S(1)}, u32[]{:S(2)}, u32[]{:S(2)}) %collective-permute-start.8) | collective-permute-done | bytes 524320 | tf_op jit(solution)/shard_map/ppermute | solution.py:122
  74.7 2.0 collective-permute-start.14
  76.6 1.5 collective-permute-start.16
  78.2 5.6 %collective-permute-start.15 = (bf16[512,1024]{1,0:T(8,128)(2,1)S(1)}, bf16[512,1024]{1,0:T(8,128)(2,1)S(1)}, u32[]{:S(2)}, u32[]{:S(2)}) collective-permute-start(bf16[512,1024]{1,0:T(8,128)(2,1)S(1)} %collective-permute-done.9), channel_id=1, source_target_pairs={{0,16},{1,17},{2,18},{3,19},{4,20},{5,21},{6,22},{7,23},{8,56},{9,... | collective-permute-start | bytes 3145736 | tf_op jit(solution)/shard_map/ppermute | solution.py:122
  84.9 7.4 %collective-permute-done.16 = bf16[512,1024]{1,0:T(8,128)(2,1)S(1)} collective-permute-done((bf16[512,1024]{1,0:T(8,128)(2,1)S(1)}, bf16[512,1024]{1,0:T(8,128)(2,1)S(1)}, u32[]{:S(2)}, u32[]{:S(2)}) %collective-permute-start.16) | collective-permute-done | bytes 1048608 | tf_op jit(solution)/shard_map/ppermute | solution.py:122
  92.3 3.2 %collective-permute-done.15 = bf16[512,1024]{1,0:T(8,128)(2,1)S(1)} collective-permute-done((bf16[512,1024]{1,0:T(8,128)(2,1)S(1)}, bf16[512,1024]{1,0:T(8,128)(2,1)S(1)}, u32[]{:S(2)}, u32[]{:S(2)}) %collective-permute-start.15) | collective-permute-done | bytes 1048608 | tf_op jit(solution)/shard_map/ppermute | solution.py:122
  97.6 11.2 %convolution_convert_fusion.refs_1_ = bf16[1024,4096]{1,0:T(8,128)(2,1)} fusion(bf16[1024,1024]{1,0:T(8,128)(2,1)S(1)} %shard_map.69, bf16[4096,1024]{1,0:T(8,128)(2,1)S(1)} %select_dynamic-update-slice_fusion.refs_0_), kind=kOutput, calls=%fused_computation | convolution fusion | flops 8594128896 | bytes 18874368 | tf_op jit(solution)/shard_map/dot_general | solution.py:110
  108.8 3.3 %copy-done.2 = bf16[4096,1024]{1,0:T(8,128)(2,1)} copy-done((bf16[4096,1024]{1,0:T(8,128)(2,1)}, bf16[4096,1024]{1,0:T(8,128)(2,1)S(1)}, u32[]{:S(2)}) %copy-start.2) | copy-done | bytes 8388632
  112.2 2.7 %multiply_convert_fusion.6.refs_3_ = bf16[512,1024]{1,0:T(8,128)(2,1)S(1)} fusion(bf16[1024,1024]{1,0:T(8,128)(2,1)S(1)} %shard_map.69, bf16[1024,4096]{1,0:T(8,128)(2,1)} %all-gather.2.cloned.1.call-done), kind=kOutput, calls=%fused_computation.13 | convolution fusion | flops 1074790400 | bytes 4194304 | tf_op jit(solution)/shard_map/dot_general | solution.py:110
  115.0 2.7 %multiply_convert_fusion.7.refs_2_ = bf16[512,1024]{1,0:T(8,128)(2,1)S(1)} fusion(bf16[1024,1024]{1,0:T(8,128)(2,1)S(1)} %shard_map.69, bf16[1024,4096]{1,0:T(8,128)(2,1)} %all-gather.2.cloned.1.call-done), kind=kOutput, calls=%fused_computation.14 | convolution fusion | flops 1074790400 | bytes 4194304 | tf_op jit(solution)/shard_map/dot_general | solution.py:110
  118.0 3.7 %multiply_convert_fusion.4.refs_5_ = bf16[512,1024]{1,0:T(8,128)(2,1)} fusion(bf16[1024,1024]{1,0:T(8,128)(2,1)S(1)} %shard_map.69, bf16[1024,4096]{1,0:T(8,128)(2,1)} %all-gather.2.cloned.1.call-done, s32[]{:T(128)S(6)} %select_n.87), kind=kOutput, calls=%fused_computation.11 | convolution fusion | flops 1074790400 | bytes 4194308 | tf_op jit(solution)/shard_map/dot_general | solution.py:110
  121.6 2.7 %multiply_convert_fusion.5.refs_4_ = bf16[512,1024]{1,0:T(8,128)(2,1)S(1)} fusion(bf16[1024,1024]{1,0:T(8,128)(2,1)S(1)} %shard_map.69, bf16[1024,4096]{1,0:T(8,128)(2,1)} %all-gather.2.cloned.1.call-done, s32[]{:T(128)S(6)} %select_n.86), kind=kOutput, calls=%fused_computation.12 | convolution fusion | flops 1074790400 | bytes 4194308 | tf_op jit(solution)/shard_map/dot_general | solution.py:110
  124.6 2.1 slice-done.3
  126.7 9.0 %convolution_convert_fusion.1.refs_1_ = bf16[1024,1024]{1,0:T(8,128)(2,1)S(1)} fusion(bf16[1024,4096]{1,0:T(8,128)(2,1)S(1)} %bitcast.34, bf16[4096,1024]{1,0:T(8,128)(2,1)S(1)} %shard_map.70), kind=kOutput, calls=%fused_computation.15 | convolution fusion | flops 8590983168 | bytes 18874368 | tf_op jit(solution)/shard_map/dot_general | solution.py:110
  135.7 2.6 %collective-permute-start.22 = (bf16[512,1024]{1,0:T(8,128)(2,1)}, bf16[512,1024]{1,0:T(8,128)(2,1)}, u32[]{:S(2)}, u32[]{:S(2)}) collective-permute-start(bf16[512,1024]{1,0:T(8,128)(2,1)} %multiply_convert_fusion.4.refs_5_), channel_id=1, source_target_pairs={{0,1},{1,64},{2,3},{3,66},{4,5},{5,68},{6,7},{7,70},{8,73},{9,8},{... | collective-permute-start | bytes 3145736 | tf_op jit(solution)/shard_map/ppermute | solution.py:122
  139.6 1.5 add_convert_fusion.2
  142.3 3.2 %collective-permute-start.17 = (bf16[512,1024]{1,0:T(8,128)(2,1)S(1)}, bf16[512,1024]{1,0:T(8,128)(2,1)}, u32[]{:S(2)}, u32[]{:S(2)}) collective-permute-start(bf16[512,1024]{1,0:T(8,128)(2,1)S(1)} %multiply_convert_fusion.5.refs_4_), channel_id=1, source_target_pairs={{0,16},{1,17},{2,18},{3,19},{4,20},{5,21},{6,22},{7,23},{8,56},{9,... | collective-permute-start | bytes 3145736 | tf_op jit(solution)/shard_map/ppermute | solution.py:122
  145.5 1.4 add_convert_fusion.4
  147.0 2.3 %multiply_convert_fusion.1 = bf16[512,1024]{1,0:T(8,128)(2,1)} fusion(bf16[1024,1024]{1,0:T(8,128)(2,1)S(1)} %shard_map.69, bf16[1024,4096]{1,0:T(8,128)(2,1)S(1)} %bitcast.34), kind=kOutput, calls=%fused_computation.6 | convolution fusion | flops 1074790400 | bytes 4194304 | tf_op jit(solution)/shard_map/dot_general | solution.py:110
  149.2 9.2 %all-to-all-start = ((bf16[8,128,1024]{2,1,0:T(8,128)(2,1)}), bf16[8,128,1024]{2,1,0:T(8,128)(2,1)}, u32[]{:S(2)}, u32[]{:S(2)}) async-start(bf16[8,128,1024]{2,1,0:T(8,128)(2,1)} %bitcast.31), calls=%async_computation | async-start | bytes 4194304 | tf_op jit(solution)/shard_map/all_to_all | solution.py:206
  158.5 2.6 %multiply_convert_fusion.3 = bf16[512,1024]{1,0:T(8,128)(2,1)S(1)} fusion(bf16[1024,1024]{1,0:T(8,128)(2,1)S(1)} %shard_map.69, bf16[1024,4096]{1,0:T(8,128)(2,1)} %all-gather.2.cloned.1.call-done), kind=kOutput, calls=%fused_computation.10 | convolution fusion | flops 1074790400 | bytes 4194304 | tf_op jit(solution)/shard_map/dot_general | solution.py:110
  161.1 6.0 %collective-permute-done.24 = bf16[512,1024]{1,0:T(8,128)(2,1)} collective-permute-done((bf16[512,1024]{1,0:T(8,128)(2,1)}, bf16[512,1024]{1,0:T(8,128)(2,1)}, u32[]{:S(2)}, u32[]{:S(2)}) %collective-permute-start.24) | collective-permute-done | bytes 1048608 | tf_op jit(solution)/shard_map/ppermute | solution.py:122
  167.1 2.0 add_convert_fusion.1
  169.5 3.7 %collective-permute-done.19 = bf16[512,1024]{1,0:T(8,128)(2,1)} collective-permute-done((bf16[512,1024]{1,0:T(8,128)(2,1)}, bf16[512,1024]{1,0:T(8,128)(2,1)}, u32[]{:S(2)}, u32[]{:S(2)}) %collective-permute-start.19) | collective-permute-done | bytes 1048608 | tf_op jit(solution)/shard_map/ppermute | solution.py:122
  173.2 2.0 add_convert_fusion.3
  175.3 2.7 %collective-permute-start.27 = (bf16[128,1024]{1,0:T(8,128)(2,1)S(1)}, bf16[128,1024]{1,0:T(8,128)(2,1)S(1)}, u32[]{:S(2)}, u32[]{:S(2)}) collective-permute-start(bf16[128,1024]{1,0:T(8,128)(2,1)S(1)} %get-tuple-element.183), channel_id=1, source_target_pairs={{0,1},{1,64},{2,3},{3,66},{4,5},{5,68},{6,7},{7,70},{8,73},{9,8},{... | collective-permute-start | bytes 786440 | tf_op jit(solution)/shard_map/ppermute | solution.py:122
  180.3 3.0 %collective-permute-done.20 = bf16[128,1024]{1,0:T(8,128)(2,1)S(1)} collective-permute-done((bf16[128,1024]{1,0:T(8,128)(2,1)S(1)}, bf16[128,1024]{1,0:T(8,128)(2,1)S(1)}, u32[]{:S(2)}, u32[]{:S(2)}) %collective-permute-start.20) | collective-permute-done | bytes 262176 | tf_op jit(solution)/shard_map/ppermute | solution.py:122
  184.9 2.0 convert_bitcast_fusion
  188.1 2.6 %collective-permute-done.21 = bf16[128,1024]{1,0:T(8,128)(2,1)S(1)} collective-permute-done((bf16[128,1024]{1,0:T(8,128)(2,1)}, bf16[128,1024]{1,0:T(8,128)(2,1)S(1)}, u32[]{:S(2)}, u32[]{:S(2)}) %collective-permute-start.21) | collective-permute-done | bytes 262176 | tf_op jit(solution)/shard_map/ppermute | solution.py:122
  192.0 2.5 %collective-permute-start.29 = (bf16[256,1024]{1,0:T(8,128)(2,1)S(1)}, bf16[256,1024]{1,0:T(8,128)(2,1)S(1)}, u32[]{:S(2)}, u32[]{:S(2)}) collective-permute-start(bf16[256,1024]{1,0:T(8,128)(2,1)S(1)} %pad_maximum_fusion.3), channel_id=1, source_target_pairs={{0,0},{1,8},{2,2},{3,10},{4,4},{5,12},{6,6},{7,14},{8,1},{9,9},{10... | collective-permute-start | bytes 1572872 | tf_op jit(solution)/shard_map/ppermute | solution.py:122
  194.5 1.8 add_convert_fusion
  196.3 6.2 %collective-permute-done.29 = bf16[256,1024]{1,0:T(8,128)(2,1)S(1)} collective-permute-done((bf16[256,1024]{1,0:T(8,128)(2,1)S(1)}, bf16[256,1024]{1,0:T(8,128)(2,1)S(1)}, u32[]{:S(2)}, u32[]{:S(2)}) %collective-permute-start.29) | collective-permute-done | bytes 524320 | tf_op jit(solution)/shard_map/ppermute | solution.py:122
  203.8 1.8 shard_map.71
  (119 shorter events, 24.4 us)
Async XLA Ops:
  7.2 8.0 %copy-start.4 = (bf16[128,8192]{1,0:T(8,128)(2,1)S(1)}, bf16[128,8192]{1,0:T(8,128)(2,1)}, u32[]{:S(2)}) copy-start(bf16[128,8192]{1,0:T(8,128)(2,1)} %cotangent.1) | copy-start | bytes 6291460
  7.2 105.0 %all-gather.2.cloned.1.call-start = ((), (), s32[]{:S(2)}) async-start(), calls=%async_computation.2 | async-start | bytes 9437184 | tf_op jit(solution)/shard_map/all_gather | solution.py:143
  10.5 192.0 %reduce-scatter.2.cloned.1.call-start = ((), (), s32[]{:S(2)}) async-start(), calls=%async_computation.3 | async-start | bytes 9437184 | tf_op jit(solution)/shard_map/reduce_scatter | solution.py:202
  10.5 12.0 %collective-permute-start = (bf16[256,1024]{1,0:T(8,128)(2,1)}, bf16[256,1024]{1,0:T(8,128)(2,1)S(1)}, u32[]{:S(2)}, u32[]{:S(2)}) collective-permute-start(bf16[256,1024]{1,0:T(8,128)(2,1)} %param.6), channel_id=1, source_target_pairs={{0,0},{1,8},{2,2},{3,10},{4,4},{5,12},{6,6},{7,14},{8,1},{9,9},{10... | collective-permute-start | bytes 1572872 | tf_op jit(solution)/shard_map/ppermute | solution.py:122
  17.6 18.6 %collective-permute-start.3 = (bf16[2,128,1024]{2,1,0:T(8,128)(2,1)}, bf16[2,128,1024]{2,1,0:T(8,128)(2,1)S(1)}, u32[]{:S(2)}, u32[]{:S(2)}) collective-permute-start(bf16[2,128,1024]{2,1,0:T(8,128)(2,1)} %get-tuple-element.106), channel_id=1, source_target_pairs={{0,2},{1,3},{2,4},{3,5},{4,6},{5,7},{6,0},{7,1},{8,14},{9,15},{10,... | collective-permute-start | bytes 1572872 | tf_op jit(solution)/shard_map/ppermute | solution.py:122
  22.5 9.3 %copy-start.12 = (bf16[256,1024]{1,0:T(8,128)(2,1)}, bf16[256,1024]{1,0:T(8,128)(2,1)S(1)}, u32[]{:S(2)}) copy-start(bf16[256,1024]{1,0:T(8,128)(2,1)S(1)} %collective-permute-done) | copy-start | bytes 1572868
  23.4 19.7 %copy-start.15 = (bf16[128,1024]{1,0:T(8,128)(2,1)}, bf16[128,1024]{1,0:T(8,128)(2,1)S(1)}, u32[]{:S(2)}) copy-start(bf16[128,1024]{1,0:T(8,128)(2,1)S(1)} %get-tuple-element.111) | copy-start | bytes 786436
  23.4 5.6 %collective-permute-start.1 = (bf16[128,1024]{1,0:T(8,128)(2,1)S(1)}, bf16[128,1024]{1,0:T(8,128)(2,1)S(1)}, u32[]{:S(2)}, u32[]{:S(2)}) collective-permute-start(bf16[128,1024]{1,0:T(8,128)(2,1)S(1)} %get-tuple-element.111), channel_id=1, source_target_pairs={{0,1},{1,64},{2,3},{3,66},{4,5},{5,68},{6,7},{7,70},{8,73},{9,8},{... | collective-permute-start | bytes 786440 | tf_op jit(solution)/shard_map/ppermute | solution.py:122
  23.4 11.2 %collective-permute-start.2 = (bf16[128,1024]{1,0:T(8,128)(2,1)S(1)}, bf16[128,1024]{1,0:T(8,128)(2,1)S(1)}, u32[]{:S(2)}, u32[]{:S(2)}) collective-permute-start(bf16[128,1024]{1,0:T(8,128)(2,1)S(1)} %get-tuple-element.118), channel_id=1, source_target_pairs={{0,16},{1,17},{2,18},{3,19},{4,20},{5,21},{6,22},{7,23},{8,56},{9,... | collective-permute-start | bytes 786440 | tf_op jit(solution)/shard_map/ppermute | solution.py:122
  27.1 13.0 %collective-permute-start.4 = (bf16[128,1024]{1,0:T(8,128)(2,1)S(1)}, bf16[128,1024]{1,0:T(8,128)(2,1)S(1)}, u32[]{:S(2)}, u32[]{:S(2)}) collective-permute-start(bf16[128,1024]{1,0:T(8,128)(2,1)S(1)} %get-tuple-element.111), channel_id=1, source_target_pairs={{0,65},{1,0},{2,67},{3,2},{4,69},{5,4},{6,71},{7,6},{8,9},{9,72},{... | collective-permute-start | bytes 786440 | tf_op jit(solution)/shard_map/ppermute | solution.py:122
  29.0 11.8 %collective-permute-start.5 = (bf16[128,1024]{1,0:T(8,128)(2,1)S(1)}, bf16[128,1024]{1,0:T(8,128)(2,1)S(1)}, u32[]{:S(2)}, u32[]{:S(2)}) collective-permute-start(bf16[128,1024]{1,0:T(8,128)(2,1)S(1)} %get-tuple-element.111), channel_id=1, source_target_pairs={{0,64},{1,65},{2,66},{3,67},{4,68},{5,69},{6,70},{7,71},{8,72},{9,... | collective-permute-start | bytes 786440 | tf_op jit(solution)/shard_map/ppermute | solution.py:122
  31.8 26.6 %collective-permute-start.11 = (bf16[2,128,1024]{2,1,0:T(8,128)(2,1)}, bf16[2,128,1024]{2,1,0:T(8,128)(2,1)S(1)}, u32[]{:S(2)}, u32[]{:S(2)}) collective-permute-start(bf16[2,128,1024]{2,1,0:T(8,128)(2,1)} %get-tuple-element.134), channel_id=1, source_target_pairs={{0,4},{1,5},{2,6},{3,7},{4,0},{5,1},{6,2},{7,3},{8,12},{9,13},{10,... | collective-permute-start | bytes 1572872 | tf_op jit(solution)/shard_map/ppermute | solution.py:122
  34.5 8.5 %copy-start.17 = (bf16[128,1024]{1,0:T(8,128)(2,1)}, bf16[128,1024]{1,0:T(8,128)(2,1)S(1)}, u32[]{:S(2)}) copy-start(bf16[128,1024]{1,0:T(8,128)(2,1)S(1)} %collective-permute-done.2) | copy-start | bytes 786436
  34.5 9.9 %collective-permute-start.6 = (bf16[128,1024]{1,0:T(8,128)(2,1)S(1)}, bf16[128,1024]{1,0:T(8,128)(2,1)S(1)}, u32[]{:S(2)}, u32[]{:S(2)}) collective-permute-start(bf16[128,1024]{1,0:T(8,128)(2,1)S(1)} %get-tuple-element.118), channel_id=1, source_target_pairs={{0,48},{1,49},{2,50},{3,51},{4,52},{5,53},{6,54},{7,55},{8,24},{9,... | collective-permute-start | bytes 786440 | tf_op jit(solution)/shard_map/ppermute | solution.py:122
  36.2 11.1 %collective-permute-start.7 = (bf16[128,1024]{1,0:T(8,128)(2,1)S(1)}, bf16[128,1024]{1,0:T(8,128)(2,1)S(1)}, u32[]{:S(2)}, u32[]{:S(2)}) collective-permute-start(bf16[128,1024]{1,0:T(8,128)(2,1)S(1)} %get-tuple-element.118), channel_id=1, source_target_pairs={{0,32},{1,33},{2,34},{3,35},{4,36},{5,37},{6,38},{7,39},{8,40},{9,... | collective-permute-start | bytes 786440 | tf_op jit(solution)/shard_map/ppermute | solution.py:122
  43.1 7.2 %copy-start.10 = (bf16[2,128,1024]{2,1,0:T(8,128)(2,1)S(1)}, bf16[2,128,1024]{2,1,0:T(8,128)(2,1)}, u32[]{:S(2)}) copy-start(bf16[2,128,1024]{2,1,0:T(8,128)(2,1)} %copy-done.9) | copy-start | bytes 1572868
  43.1 40.7 %copy-start.1 = (bf16[4096,1024]{1,0:T(8,128)(2,1)S(1)}, bf16[4096,1024]{1,0:T(8,128)(2,1)}, u32[]{:S(2)}) copy-start(bf16[4096,1024]{1,0:T(8,128)(2,1)} %get-tuple-element.179) | copy-start | bytes 25165828
  48.4 28.3 %collective-permute-start.10 = (bf16[512,1024]{1,0:T(8,128)(2,1)S(1)}, bf16[512,1024]{1,0:T(8,128)(2,1)S(1)}, u32[]{:S(2)}, u32[]{:S(2)}) collective-permute-start(bf16[512,1024]{1,0:T(8,128)(2,1)S(1)} %pad_maximum_fusion.1), channel_id=1, source_target_pairs={{0,1},{1,64},{2,3},{3,66},{4,5},{5,68},{6,7},{7,70},{8,73},{9,8},{... | collective-permute-start | bytes 3145736 | tf_op jit(solution)/shard_map/ppermute | solution.py:122
  49.0 29.2 %collective-permute-start.9 = (bf16[512,1024]{1,0:T(8,128)(2,1)S(1)}, bf16[512,1024]{1,0:T(8,128)(2,1)S(1)}, u32[]{:S(2)}, u32[]{:S(2)}) collective-permute-start(bf16[512,1024]{1,0:T(8,128)(2,1)S(1)} %pad_maximum_fusion), channel_id=1, source_target_pairs={{0,16},{1,17},{2,18},{3,19},{4,20},{5,21},{6,22},{7,23},{8,56},{9,... | collective-permute-start | bytes 3145736 | tf_op jit(solution)/shard_map/ppermute | solution.py:122
  50.3 24.3 %collective-permute-start.8 = (bf16[2,128,1024]{2,1,0:T(8,128)(2,1)S(1)}, bf16[2,128,1024]{2,1,0:T(8,128)(2,1)S(1)}, u32[]{:S(2)}, u32[]{:S(2)}) collective-permute-start(bf16[2,128,1024]{2,1,0:T(8,128)(2,1)S(1)} %copy-done.10), channel_id=1, source_target_pairs={{0,6},{1,7},{2,0},{3,1},{4,2},{5,3},{6,4},{7,5},{8,10},{9,11},{10,... | collective-permute-start | bytes 1572872 | tf_op jit(solution)/shard_map/ppermute | solution.py:122
  58.4 16.2 %copy-start.5 = (bf16[2,128,1024]{2,1,0:T(8,128)(2,1)}, bf16[2,128,1024]{2,1,0:T(8,128)(2,1)S(1)}, u32[]{:S(2)}) copy-start(bf16[2,128,1024]{2,1,0:T(8,128)(2,1)S(1)} %collective-permute-done.11.across) | copy-start | bytes 1572868
  58.5 25.3 %collective-permute-start.12 = (bf16[512,1024]{1,0:T(8,128)(2,1)S(1)}, bf16[512,1024]{1,0:T(8,128)(2,1)S(1)}, u32[]{:S(2)}, u32[]{:S(2)}) collective-permute-start(bf16[512,1024]{1,0:T(8,128)(2,1)S(1)} %pad_maximum_fusion), channel_id=1, source_target_pairs={{0,48},{1,49},{2,50},{3,51},{4,52},{5,53},{6,54},{7,55},{8,24},{9,... | collective-permute-start | bytes 3145736 | tf_op jit(solution)/shard_map/ppermute | solution.py:122
  59.3 24.5 %collective-permute-start.13 = (bf16[512,1024]{1,0:T(8,128)(2,1)S(1)}, bf16[512,1024]{1,0:T(8,128)(2,1)S(1)}, u32[]{:S(2)}, u32[]{:S(2)}) collective-permute-start(bf16[512,1024]{1,0:T(8,128)(2,1)S(1)} %pad_maximum_fusion.1), channel_id=1, source_target_pairs={{0,65},{1,0},{2,67},{3,2},{4,69},{5,4},{6,71},{7,6},{8,9},{9,72},{... | collective-permute-start | bytes 3145736 | tf_op jit(solution)/shard_map/ppermute | solution.py:122
  74.7 9.5 %collective-permute-start.14 = (bf16[512,1024]{1,0:T(8,128)(2,1)S(1)}, bf16[512,1024]{1,0:T(8,128)(2,1)S(1)}, u32[]{:S(2)}, u32[]{:S(2)}) collective-permute-start(bf16[512,1024]{1,0:T(8,128)(2,1)S(1)} %pad_maximum_fusion.2), channel_id=1, source_target_pairs={{0,8},{1,9},{2,10},{3,11},{4,12},{5,13},{6,14},{7,15},{8,0},{9,1},... | collective-permute-start | bytes 3145736 | tf_op jit(solution)/shard_map/ppermute | solution.py:122
  76.6 7.6 %copy-start.6 = (bf16[2,128,1024]{2,1,0:T(8,128)(2,1)S(1)}, bf16[2,128,1024]{2,1,0:T(8,128)(2,1)}, u32[]{:S(2)}) copy-start(bf16[2,128,1024]{2,1,0:T(8,128)(2,1)} %copy-done.5) | copy-start | bytes 1572868
  76.6 15.7 %collective-permute-start.16 = (bf16[512,1024]{1,0:T(8,128)(2,1)S(1)}, bf16[512,1024]{1,0:T(8,128)(2,1)S(1)}, u32[]{:S(2)}, u32[]{:S(2)}) collective-permute-start(bf16[512,1024]{1,0:T(8,128)(2,1)S(1)} %collective-permute-done.10), channel_id=1, source_target_pairs={{0,1},{1,64},{2,3},{3,66},{4,5},{5,68},{6,7},{7,70},{8,73},{9,8},{... | collective-permute-start | bytes 3145736 | tf_op jit(solution)/shard_map/ppermute | solution.py:122
  78.2 17.4 %collective-permute-start.15 = (bf16[512,1024]{1,0:T(8,128)(2,1)S(1)}, bf16[512,1024]{1,0:T(8,128)(2,1)S(1)}, u32[]{:S(2)}, u32[]{:S(2)}) collective-permute-start(bf16[512,1024]{1,0:T(8,128)(2,1)S(1)} %collective-permute-done.9), channel_id=1, source_target_pairs={{0,16},{1,17},{2,18},{3,19},{4,20},{5,21},{6,22},{7,23},{8,56},{9,... | collective-permute-start | bytes 3145736 | tf_op jit(solution)/shard_map/ppermute | solution.py:122
  108.8 3.3 %copy-start.2 = (bf16[4096,1024]{1,0:T(8,128)(2,1)}, bf16[4096,1024]{1,0:T(8,128)(2,1)S(1)}, u32[]{:S(2)}) copy-start(bf16[4096,1024]{1,0:T(8,128)(2,1)S(1)} %select_dynamic-update-slice_fusion.refs_0_) | copy-start | bytes 25165828
  112.2 12.1 %slice-start = ((s8[8388608]{0:T(1024)(128)(4,1)}), s8[4194304]{0:T(1024)(128)(4,1)S(1)}, s32[]{:S(2)}) async-start(s8[8388608]{0:T(1024)(128)(4,1)} %bitcast.29), calls=%async_computation.4 | async-start | bytes 8388608
  114.9 9.5 %slice-start.1 = ((s8[8388608]{0:T(1024)(128)(4,1)}), s8[4194304]{0:T(1024)(128)(4,1)S(1)}, s32[]{:S(2)}) async-start(s8[8388608]{0:T(1024)(128)(4,1)} %bitcast.29), calls=%async_computation.5 | async-start | bytes 8388608
  114.9 24.7 %collective-permute-start.23 = (bf16[512,1024]{1,0:T(8,128)(2,1)S(1)}, bf16[512,1024]{1,0:T(8,128)(2,1)S(1)}, u32[]{:S(2)}, u32[]{:S(2)}) collective-permute-start(bf16[512,1024]{1,0:T(8,128)(2,1)S(1)} %multiply_convert_fusion.6.refs_3_), channel_id=1, source_target_pairs={{0,65},{1,0},{2,67},{3,2},{4,69},{5,4},{6,71},{7,6},{8,9},{9,72},{... | collective-permute-start | bytes 3145736 | tf_op jit(solution)/shard_map/ppermute | solution.py:122
  117.6 27.9 %collective-permute-start.18 = (bf16[512,1024]{1,0:T(8,128)(2,1)S(1)}, bf16[512,1024]{1,0:T(8,128)(2,1)S(1)}, u32[]{:S(2)}, u32[]{:S(2)}) collective-permute-start(bf16[512,1024]{1,0:T(8,128)(2,1)S(1)} %multiply_convert_fusion.7.refs_2_), channel_id=1, source_target_pairs={{0,48},{1,49},{2,50},{3,51},{4,52},{5,53},{6,54},{7,55},{8,24},{9,... | collective-permute-start | bytes 3145736 | tf_op jit(solution)/shard_map/ppermute | solution.py:122
  117.9 6.4 %copy-start.3 = (bf16[4096,1024]{1,0:T(8,128)(2,1)S(1)}, bf16[4096,1024]{1,0:T(8,128)(2,1)}, u32[]{:S(2)}) copy-start(bf16[4096,1024]{1,0:T(8,128)(2,1)} %copy-done.2) | copy-start | bytes 25165828
  135.7 9.9 %copy-start = (bf16[1024,1024]{1,0:T(8,128)(2,1)}, bf16[1024,1024]{1,0:T(8,128)(2,1)S(1)}, u32[]{:S(2)}) copy-start(bf16[1024,1024]{1,0:T(8,128)(2,1)S(1)} %convolution_convert_fusion.1.refs_1_) | copy-start | bytes 6291460
  135.7 25.4 %collective-permute-start.22 = (bf16[512,1024]{1,0:T(8,128)(2,1)}, bf16[512,1024]{1,0:T(8,128)(2,1)}, u32[]{:S(2)}, u32[]{:S(2)}) collective-permute-start(bf16[512,1024]{1,0:T(8,128)(2,1)} %multiply_convert_fusion.4.refs_5_), channel_id=1, source_target_pairs={{0,1},{1,64},{2,3},{3,66},{4,5},{5,68},{6,7},{7,70},{8,73},{9,8},{... | collective-permute-start | bytes 3145736 | tf_op jit(solution)/shard_map/ppermute | solution.py:122
  141.0 26.1 %collective-permute-start.24 = (bf16[512,1024]{1,0:T(8,128)(2,1)}, bf16[512,1024]{1,0:T(8,128)(2,1)}, u32[]{:S(2)}, u32[]{:S(2)}) collective-permute-start(bf16[512,1024]{1,0:T(8,128)(2,1)} %add_convert_fusion.2), channel_id=1, source_target_pairs={{0,65},{1,0},{2,67},{3,2},{4,69},{5,4},{6,71},{7,6},{8,9},{9,72},{... | collective-permute-start | bytes 3145736 | tf_op jit(solution)/shard_map/ppermute | solution.py:122
  142.3 27.2 %collective-permute-start.17 = (bf16[512,1024]{1,0:T(8,128)(2,1)S(1)}, bf16[512,1024]{1,0:T(8,128)(2,1)}, u32[]{:S(2)}, u32[]{:S(2)}) collective-permute-start(bf16[512,1024]{1,0:T(8,128)(2,1)S(1)} %multiply_convert_fusion.5.refs_4_), channel_id=1, source_target_pairs={{0,16},{1,17},{2,18},{3,19},{4,20},{5,21},{6,22},{7,23},{8,56},{9,... | collective-permute-start | bytes 3145736 | tf_op jit(solution)/shard_map/ppermute | solution.py:122
  147.0 26.2 %collective-permute-start.19 = (bf16[512,1024]{1,0:T(8,128)(2,1)}, bf16[512,1024]{1,0:T(8,128)(2,1)}, u32[]{:S(2)}, u32[]{:S(2)}) collective-permute-start(bf16[512,1024]{1,0:T(8,128)(2,1)} %add_convert_fusion.4), channel_id=1, source_target_pairs={{0,48},{1,49},{2,50},{3,51},{4,52},{5,53},{6,54},{7,55},{8,24},{9,... | collective-permute-start | bytes 3145736 | tf_op jit(solution)/shard_map/ppermute | solution.py:122
  149.2 35.7 %all-to-all-start = ((bf16[8,128,1024]{2,1,0:T(8,128)(2,1)}), bf16[8,128,1024]{2,1,0:T(8,128)(2,1)}, u32[]{:S(2)}, u32[]{:S(2)}) async-start(bf16[8,128,1024]{2,1,0:T(8,128)(2,1)} %bitcast.31), calls=%async_computation | async-start | bytes 4194304 | tf_op jit(solution)/shard_map/all_to_all | solution.py:206
  158.5 8.6 %copy-start.14 = (bf16[512,1024]{1,0:T(8,128)(2,1)S(1)}, bf16[512,1024]{1,0:T(8,128)(2,1)}, u32[]{:S(2)}) copy-start(bf16[512,1024]{1,0:T(8,128)(2,1)} %multiply_convert_fusion.1) | copy-start | bytes 3145732
  169.1 9.4 %collective-permute-start.25 = (bf16[128,1024]{1,0:T(8,128)(2,1)S(1)}, bf16[128,1024]{1,0:T(8,128)(2,1)S(1)}, u32[]{:S(2)}, u32[]{:S(2)}) collective-permute-start(bf16[128,1024]{1,0:T(8,128)(2,1)S(1)} %get-tuple-element.185), channel_id=1, source_target_pairs={{0,48},{1,49},{2,50},{3,51},{4,52},{5,53},{6,54},{7,55},{8,24},{9,... | collective-permute-start | bytes 786440 | tf_op jit(solution)/shard_map/ppermute | solution.py:122
  175.2 8.1 %collective-permute-start.20 = (bf16[128,1024]{1,0:T(8,128)(2,1)S(1)}, bf16[128,1024]{1,0:T(8,128)(2,1)S(1)}, u32[]{:S(2)}, u32[]{:S(2)}) collective-permute-start(bf16[128,1024]{1,0:T(8,128)(2,1)S(1)} %get-tuple-element.184), channel_id=1, source_target_pairs={{0,65},{1,0},{2,67},{3,2},{4,69},{5,4},{6,71},{7,6},{8,9},{9,72},{... | collective-permute-start | bytes 786440 | tf_op jit(solution)/shard_map/ppermute | solution.py:122
  175.3 12.0 %collective-permute-start.27 = (bf16[128,1024]{1,0:T(8,128)(2,1)S(1)}, bf16[128,1024]{1,0:T(8,128)(2,1)S(1)}, u32[]{:S(2)}, u32[]{:S(2)}) collective-permute-start(bf16[128,1024]{1,0:T(8,128)(2,1)S(1)} %get-tuple-element.183), channel_id=1, source_target_pairs={{0,1},{1,64},{2,3},{3,66},{4,5},{5,68},{6,7},{7,70},{8,73},{9,8},{... | collective-permute-start | bytes 786440 | tf_op jit(solution)/shard_map/ppermute | solution.py:122
  178.0 9.4 %collective-permute-start.28 = (bf16[128,1024]{1,0:T(8,128)(2,1)S(1)}, bf16[128,1024]{1,0:T(8,128)(2,1)S(1)}, u32[]{:S(2)}, u32[]{:S(2)}) collective-permute-start(bf16[128,1024]{1,0:T(8,128)(2,1)S(1)} %get-tuple-element.186), channel_id=1, source_target_pairs={{0,16},{1,17},{2,18},{3,19},{4,20},{5,21},{6,22},{7,23},{8,56},{9,... | collective-permute-start | bytes 786440 | tf_op jit(solution)/shard_map/ppermute | solution.py:122
  179.3 8.8 %collective-permute-start.26 = (bf16[128,1024]{1,0:T(8,128)(2,1)}, bf16[128,1024]{1,0:T(8,128)(2,1)}, u32[]{:S(2)}, u32[]{:S(2)}) collective-permute-start(bf16[128,1024]{1,0:T(8,128)(2,1)} %add_convert_fusion.7), channel_id=1, source_target_pairs={{0,48},{1,49},{2,50},{3,51},{4,52},{5,53},{6,54},{7,55},{8,24},{9,... | collective-permute-start | bytes 786440 | tf_op jit(solution)/shard_map/ppermute | solution.py:122
  184.1 6.6 %collective-permute-start.21 = (bf16[128,1024]{1,0:T(8,128)(2,1)}, bf16[128,1024]{1,0:T(8,128)(2,1)S(1)}, u32[]{:S(2)}, u32[]{:S(2)}) collective-permute-start(bf16[128,1024]{1,0:T(8,128)(2,1)} %add_convert_fusion.8), channel_id=1, source_target_pairs={{0,65},{1,0},{2,67},{3,2},{4,69},{5,4},{6,71},{7,6},{8,9},{9,72},{... | collective-permute-start | bytes 786440 | tf_op jit(solution)/shard_map/ppermute | solution.py:122
  187.3 7.2 %copy-start.11 = (bf16[128,8192]{1,0:T(8,128)(2,1)S(1)}, bf16[128,8192]{1,0:T(8,128)(2,1)}, u32[]{:S(2)}) copy-start(bf16[128,8192]{1,0:T(8,128)(2,1)} %param.5) | copy-start | bytes 6291460
  192.0 10.5 %collective-permute-start.29 = (bf16[256,1024]{1,0:T(8,128)(2,1)S(1)}, bf16[256,1024]{1,0:T(8,128)(2,1)S(1)}, u32[]{:S(2)}, u32[]{:S(2)}) collective-permute-start(bf16[256,1024]{1,0:T(8,128)(2,1)S(1)} %pad_maximum_fusion.3), channel_id=1, source_target_pairs={{0,0},{1,8},{2,2},{3,10},{4,4},{5,12},{6,6},{7,14},{8,1},{9,9},{10... | collective-permute-start | bytes 1572872 | tf_op jit(solution)/shard_map/ppermute | solution.py:122
  (7 other events, 12.0 us)
Sparse Core Ops, SparseCore 0:
  10.6 70.1 all-gather.1
  112.3 50.5 reduce-scatter.1

commit v4 on v3

--- a/solution.py
+++ b/solution.py
@@ -202,7 +202,7 @@
     grad_heads = lax.psum_scatter(act, ("x", "c"), scatter_dimension=0, tiled=True)
     weight_up, weight_lo = weight(one), weight(4 + one)
 
-    out = dot(heads, after(proj, act, *started), ((1,), (0,))).astype(BF16)
+    out = dot(heads, after(proj, *started), ((1,), (0,))).astype(BF16)
     token_proj = lax.all_to_all(out, ("x", "c"), split_axis=0, concat_axis=1, tiled=True)
     sum_up_far, sum_lo_far = after(sum_up_far, out), after(sum_lo_far, out)
     sum_up_ahead = send(add(weight_up, sum_up_far), Z_BACK)

time: 214 us -> 210 us (0.981)
  local copies, waits for them, and re-layouts: 12.6 us -> 10.4 us
    ppermute x30, waiting for transfers between devices: 62.7 us -> 57.5 us  [send(): return lax.ppermute(self.wait(value), AXES, pairs)]
    all_to_all x1, waiting for transfers between devices: 0.78 us -> 5.59 us  [per_device(): lax.all_to_all(out, ('x', 'c'), split_axis=0, concat_axis=1, tiled=True)]
    unnamed x52 -> x44, local copies, waits for them, and re-layouts: 11.4 us -> 9.12 us
    unnamed x8 -> x7, other arithmetic: 4.84 us -> 4.85 us
  transfers between devices with their start and end apart: 33 -> 33, of which waited for: 15 -> 13; matrix products, arithmetic and copies ran while one was open for 29% -> 28% of each run, Pallas kernels for 1% -> 1%
where the time goes in v4:
time: 210 us
  waiting for transfers between devices  63.2 us (30%)
  starting transfers between devices  58.9 us (28%)
  matrix products  38.4 us (18%)
  other arithmetic  18.4 us (9%)
  between operations  14.6 us (7%)
  local copies, waits for them, and re-layouts  10.4 us (5%)
  Pallas kernels  6.03 us (3%)
    ppermute x30, waiting for transfers between devices, send(): return lax.ppermute(self.wait(value), AXES, pairs)  57.5 us
    ppermute x30, starting transfers between devices, send(): return lax.ppermute(self.wait(value), AXES, pairs)  49.1 us
    dot_general x10, matrix products, dot(): return lax.dot_general(a, b, (dims, ((), ())), preferred_element_type=F32)  38.4 us
    convert_element_type x9, other arithmetic, add(): functools.reduce(lambda p, q: p + q, [t.astype(F32) for t in terms])  11.7 us
    all_to_all x1, starting transfers between devices, per_device(): lax.all_to_all(out, ('x', 'c'), split_axis=0, concat_axis=1, tiled=True)  9.75 us
    unnamed x44, local copies, waits for them, and re-layouts  9.12 us
    pallas_call x4, Pallas kernels, local(): pl.pallas_call(kernel, out_shape=jax.tree.map(lambda s: jax.ShapeDtypeStr...  6.03 us
    all_to_all x1, waiting for transfers between devices, per_device(): lax.all_to_all(out, ('x', 'c'), split_axis=0, concat_axis=1, tiled=True)  5.59 us
  transfers between devices with their start and end apart: 33, of which 13 were waited for; matrix products, arithmetic and copies ran while one was open for 28% of the time, Pallas kernels for 1%

profile of v4, /device:TPU:1, one launch (start us, length us, event | category | flops | bytes accessed | tf_op | source)
XLA Modules:
  0.0 209.9 jit_solution(1632657977163186070)
XLA Ops:
  7.3 1.3 copy-done.6
  8.7 1.8 shard_map.68
  10.5 4.6 %collective-permute-start = (bf16[256,1024]{1,0:T(8,128)(2,1)}, bf16[256,1024]{1,0:T(8,128)(2,1)S(1)}, u32[]{:S(2)}, u32[]{:S(2)}) collective-permute-start(bf16[256,1024]{1,0:T(8,128)(2,1)} %param.6), channel_id=1, source_target_pairs={{0,0},{1,8},{2,2},{3,10},{4,4},{5,12},{6,6},{7,14},{8,1},{9,9},{10... | collective-permute-start | bytes 1572872 | tf_op jit(solution)/shard_map/ppermute | solution.py:122
  15.2 1.7 shard_map.67
  17.7 2.5 %collective-permute-start.3 = (bf16[2,128,1024]{2,1,0:T(8,128)(2,1)}, bf16[2,128,1024]{2,1,0:T(8,128)(2,1)S(1)}, u32[]{:S(2)}, u32[]{:S(2)}) collective-permute-start(bf16[2,128,1024]{2,1,0:T(8,128)(2,1)} %get-tuple-element.106), channel_id=1, source_target_pairs={{0,2},{1,3},{2,4},{3,5},{4,6},{5,7},{6,0},{7,1},{8,14},{9,15},{10,... | collective-permute-start | bytes 1572872 | tf_op jit(solution)/shard_map/ppermute | solution.py:122
  20.1 2.4 %collective-permute-done = bf16[256,1024]{1,0:T(8,128)(2,1)S(1)} collective-permute-done((bf16[256,1024]{1,0:T(8,128)(2,1)}, bf16[256,1024]{1,0:T(8,128)(2,1)S(1)}, u32[]{:S(2)}, u32[]{:S(2)}) %collective-permute-start) | collective-permute-done | bytes 524320 | tf_op jit(solution)/shard_map/ppermute | solution.py:122
  23.4 3.8 %collective-permute-start.2 = (bf16[128,1024]{1,0:T(8,128)(2,1)S(1)}, bf16[128,1024]{1,0:T(8,128)(2,1)S(1)}, u32[]{:S(2)}, u32[]{:S(2)}) collective-permute-start(bf16[128,1024]{1,0:T(8,128)(2,1)S(1)} %get-tuple-element.118), channel_id=1, source_target_pairs={{0,16},{1,17},{2,18},{3,19},{4,20},{5,21},{6,22},{7,23},{8,56},{9,... | collective-permute-start | bytes 786440 | tf_op jit(solution)/shard_map/ppermute | solution.py:122
  27.1 1.5 collective-permute-start.4
  29.0 2.8 %collective-permute-start.5 = (bf16[128,1024]{1,0:T(8,128)(2,1)S(1)}, bf16[128,1024]{1,0:T(8,128)(2,1)S(1)}, u32[]{:S(2)}, u32[]{:S(2)}) collective-permute-start(bf16[128,1024]{1,0:T(8,128)(2,1)S(1)} %get-tuple-element.111), channel_id=1, source_target_pairs={{0,64},{1,65},{2,66},{3,67},{4,68},{5,69},{6,70},{7,71},{8,72},{9,... | collective-permute-start | bytes 786440 | tf_op jit(solution)/shard_map/ppermute | solution.py:122
  31.8 2.7 %collective-permute-start.11 = (bf16[2,128,1024]{2,1,0:T(8,128)(2,1)}, bf16[2,128,1024]{2,1,0:T(8,128)(2,1)S(1)}, u32[]{:S(2)}, u32[]{:S(2)}) collective-permute-start(bf16[2,128,1024]{2,1,0:T(8,128)(2,1)} %get-tuple-element.134), channel_id=1, source_target_pairs={{0,4},{1,5},{2,6},{3,7},{4,0},{5,1},{6,2},{7,3},{8,12},{9,13},{10,... | collective-permute-start | bytes 1572872 | tf_op jit(solution)/shard_map/ppermute | solution.py:122
  34.6 1.6 collective-permute-start.6
  36.2 3.9 %collective-permute-start.7 = (bf16[128,1024]{1,0:T(8,128)(2,1)S(1)}, bf16[128,1024]{1,0:T(8,128)(2,1)S(1)}, u32[]{:S(2)}, u32[]{:S(2)}) collective-permute-start(bf16[128,1024]{1,0:T(8,128)(2,1)S(1)} %get-tuple-element.118), channel_id=1, source_target_pairs={{0,32},{1,33},{2,34},{3,35},{4,36},{5,37},{6,38},{7,39},{8,40},{9,... | collective-permute-start | bytes 786440 | tf_op jit(solution)/shard_map/ppermute | solution.py:122
  43.2 4.1 %collective-permute-done.7 = bf16[128,1024]{1,0:T(8,128)(2,1)S(1)} collective-permute-done((bf16[128,1024]{1,0:T(8,128)(2,1)S(1)}, bf16[128,1024]{1,0:T(8,128)(2,1)S(1)}, u32[]{:S(2)}, u32[]{:S(2)}) %collective-permute-start.7) | collective-permute-done | bytes 262176 | tf_op jit(solution)/shard_map/ppermute | solution.py:122
  49.0 1.3 collective-permute-start.9
  50.4 8.1 %collective-permute-done.11.across = bf16[2,128,1024]{2,1,0:T(8,128)(2,1)S(1)} collective-permute-done((bf16[2,128,1024]{2,1,0:T(8,128)(2,1)}, bf16[2,128,1024]{2,1,0:T(8,128)(2,1)S(1)}, u32[]{:S(2)}, u32[]{:S(2)}) %collective-permute-start.11) | collective-permute-done | bytes 524320 | tf_op jit(solution)/shard_map/ppermute | solution.py:122
  59.3 15.3 %collective-permute-done.8.back = bf16[2,128,1024]{2,1,0:T(8,128)(2,1)S(1)} collective-permute-done((bf16[2,128,1024]{2,1,0:T(8,128)(2,1)S(1)}, bf16[2,128,1024]{2,1,0:T(8,128)(2,1)S(1)}, u32[]{:S(2)}, u32[]{:S(2)}) %collective-permute-start.8) | collective-permute-done | bytes 524320 | tf_op jit(solution)/shard_map/ppermute | solution.py:122
  74.7 2.0 collective-permute-start.14
  76.7 1.5 collective-permute-start.16
  78.2 5.6 %collective-permute-start.15 = (bf16[512,1024]{1,0:T(8,128)(2,1)S(1)}, bf16[512,1024]{1,0:T(8,128)(2,1)S(1)}, u32[]{:S(2)}, u32[]{:S(2)}) collective-permute-start(bf16[512,1024]{1,0:T(8,128)(2,1)S(1)} %collective-permute-done.9), channel_id=1, source_target_pairs={{0,16},{1,17},{2,18},{3,19},{4,20},{5,21},{6,22},{7,23},{8,56},{9,... | collective-permute-start | bytes 3145736 | tf_op jit(solution)/shard_map/ppermute | solution.py:122
  84.9 7.4 %collective-permute-done.16 = bf16[512,1024]{1,0:T(8,128)(2,1)S(1)} collective-permute-done((bf16[512,1024]{1,0:T(8,128)(2,1)S(1)}, bf16[512,1024]{1,0:T(8,128)(2,1)S(1)}, u32[]{:S(2)}, u32[]{:S(2)}) %collective-permute-start.16) | collective-permute-done | bytes 1048608 | tf_op jit(solution)/shard_map/ppermute | solution.py:122
  92.3 3.2 %collective-permute-done.15 = bf16[512,1024]{1,0:T(8,128)(2,1)S(1)} collective-permute-done((bf16[512,1024]{1,0:T(8,128)(2,1)S(1)}, bf16[512,1024]{1,0:T(8,128)(2,1)S(1)}, u32[]{:S(2)}, u32[]{:S(2)}) %collective-permute-start.15) | collective-permute-done | bytes 1048608 | tf_op jit(solution)/shard_map/ppermute | solution.py:122
  97.6 11.1 %convolution_convert_fusion = bf16[1024,4096]{1,0:T(8,128)(2,1)} fusion(bf16[1024,1024]{1,0:T(8,128)(2,1)S(1)} %shard_map.69, bf16[4096,1024]{1,0:T(8,128)(2,1)S(1)} %select_dynamic-update-slice_fusion.refs_0_), kind=kOutput, calls=%fused_computation | convolution fusion | flops 8594128896 | bytes 18874368 | tf_op jit(solution)/shard_map/dot_general | solution.py:110
  108.8 3.3 %copy-done.2 = bf16[4096,1024]{1,0:T(8,128)(2,1)} copy-done((bf16[4096,1024]{1,0:T(8,128)(2,1)}, bf16[4096,1024]{1,0:T(8,128)(2,1)S(1)}, u32[]{:S(2)}) %copy-start.2) | copy-done | bytes 8388632
  112.2 2.7 %multiply_convert_fusion.6.refs_2_ = bf16[512,1024]{1,0:T(8,128)(2,1)S(1)} fusion(bf16[1024,1024]{1,0:T(8,128)(2,1)S(1)} %shard_map.69, bf16[1024,4096]{1,0:T(8,128)(2,1)} %all-gather.2.cloned.1.call-done), kind=kOutput, calls=%fused_computation.13 | convolution fusion | flops 1074790400 | bytes 4194304 | tf_op jit(solution)/shard_map/dot_general | solution.py:110
  115.0 3.3 %multiply_convert_fusion.7.refs_1_ = bf16[512,1024]{1,0:T(8,128)(2,1)S(1)} fusion(bf16[1024,1024]{1,0:T(8,128)(2,1)S(1)} %shard_map.69, bf16[1024,4096]{1,0:T(8,128)(2,1)} %all-gather.2.cloned.1.call-done), kind=kOutput, calls=%fused_computation.14 | convolution fusion | flops 1074790400 | bytes 4194304 | tf_op jit(solution)/shard_map/dot_general | solution.py:110
  118.6 3.5 %multiply_convert_fusion.4.refs_4_ = bf16[512,1024]{1,0:T(8,128)(2,1)} fusion(bf16[1024,1024]{1,0:T(8,128)(2,1)S(1)} %shard_map.69, bf16[1024,4096]{1,0:T(8,128)(2,1)} %all-gather.2.cloned.1.call-done, s32[]{:T(128)S(6)} %select_n.87), kind=kOutput, calls=%fused_computation.11 | convolution fusion | flops 1074790400 | bytes 4194308 | tf_op jit(solution)/shard_map/dot_general | solution.py:110
  123.4 9.0 %convolution_convert_fusion.1.refs_1_ = bf16[1024,1024]{1,0:T(8,128)(2,1)S(1)} fusion(bf16[1024,4096]{1,0:T(8,128)(2,1)S(1)} %copy-done.10, bf16[4096,1024]{1,0:T(8,128)(2,1)S(1)} %shard_map.70), kind=kOutput, calls=%fused_computation.15 | convolution fusion | flops 8590983168 | bytes 18874368 | tf_op jit(solution)/shard_map/dot_general | solution.py:110
  132.5 2.2 %collective-permute-start.22 = (bf16[512,1024]{1,0:T(8,128)(2,1)}, bf16[512,1024]{1,0:T(8,128)(2,1)}, u32[]{:S(2)}, u32[]{:S(2)}) collective-permute-start(bf16[512,1024]{1,0:T(8,128)(2,1)} %multiply_convert_fusion.4.refs_4_), channel_id=1, source_target_pairs={{0,1},{1,64},{2,3},{3,66},{4,5},{5,68},{6,7},{7,70},{8,73},{9,8},{... | collective-permute-start | bytes 3145736 | tf_op jit(solution)/shard_map/ppermute | solution.py:122
  136.0 1.5 add_convert_fusion.2
  137.5 1.3 multiply_convert_fusion.2
  138.8 3.0 %collective-permute-start.17 = (bf16[512,1024]{1,0:T(8,128)(2,1)S(1)}, bf16[512,1024]{1,0:T(8,128)(2,1)}, u32[]{:S(2)}, u32[]{:S(2)}) collective-permute-start(bf16[512,1024]{1,0:T(8,128)(2,1)S(1)} %multiply_convert_fusion.5.refs_3_), channel_id=1, source_target_pairs={{0,16},{1,17},{2,18},{3,19},{4,20},{5,21},{6,22},{7,23},{8,56},{9,... | collective-permute-start | bytes 3145736 | tf_op jit(solution)/shard_map/ppermute | solution.py:122
  141.8 1.4 add_convert_fusion.4
  143.2 2.3 %multiply_convert_fusion.1 = bf16[512,1024]{1,0:T(8,128)(2,1)} fusion(bf16[1024,1024]{1,0:T(8,128)(2,1)S(1)} %shard_map.69, bf16[1024,4096]{1,0:T(8,128)(2,1)S(1)} %copy-done.10), kind=kOutput, calls=%fused_computation.6 | convolution fusion | flops 1074790400 | bytes 4194304 | tf_op jit(solution)/shard_map/dot_general | solution.py:110
  145.5 9.8 %all-to-all-start = ((bf16[8,128,1024]{2,1,0:T(8,128)(2,1)}), bf16[8,128,1024]{2,1,0:T(8,128)(2,1)}, u32[]{:S(2)}, u32[]{:S(2)}) async-start(bf16[8,128,1024]{2,1,0:T(8,128)(2,1)} %bitcast.29), calls=%async_computation | async-start | bytes 4194304 | tf_op jit(solution)/shard_map/all_to_all | solution.py:206
  155.2 2.6 %multiply_convert_fusion.3 = bf16[512,1024]{1,0:T(8,128)(2,1)S(1)} fusion(bf16[1024,1024]{1,0:T(8,128)(2,1)S(1)} %shard_map.69, bf16[1024,4096]{1,0:T(8,128)(2,1)} %all-gather.2.cloned.1.call-done), kind=kOutput, calls=%fused_computation.10 | convolution fusion | flops 1074790400 | bytes 4194304 | tf_op jit(solution)/shard_map/dot_general | solution.py:110
  157.9 5.9 %collective-permute-done.24 = bf16[512,1024]{1,0:T(8,128)(2,1)} collective-permute-done((bf16[512,1024]{1,0:T(8,128)(2,1)}, bf16[512,1024]{1,0:T(8,128)(2,1)}, u32[]{:S(2)}, u32[]{:S(2)}) %collective-permute-start.24) | collective-permute-done | bytes 1048608 | tf_op jit(solution)/shard_map/ppermute | solution.py:122
  163.8 2.1 add_convert_fusion.1
  166.3 2.5 %collective-permute-done.19 = bf16[512,1024]{1,0:T(8,128)(2,1)} collective-permute-done((bf16[512,1024]{1,0:T(8,128)(2,1)}, bf16[512,1024]{1,0:T(8,128)(2,1)}, u32[]{:S(2)}, u32[]{:S(2)}) %collective-permute-start.19) | collective-permute-done | bytes 1048608 | tf_op jit(solution)/shard_map/ppermute | solution.py:122
  168.8 2.0 add_convert_fusion.3
  171.7 2.0 collective-permute-start.27
  173.6 1.5 collective-permute-start.28
  175.9 2.5 %collective-permute-done.20 = bf16[128,1024]{1,0:T(8,128)(2,1)S(1)} collective-permute-done((bf16[128,1024]{1,0:T(8,128)(2,1)S(1)}, bf16[128,1024]{1,0:T(8,128)(2,1)S(1)}, u32[]{:S(2)}, u32[]{:S(2)}) %collective-permute-start.20) | collective-permute-done | bytes 262176 | tf_op jit(solution)/shard_map/ppermute | solution.py:122
  179.3 5.6 %all-to-all-done = bf16[8,128,1024]{2,1,0:T(8,128)(2,1)} async-done(((bf16[8,128,1024]{2,1,0:T(8,128)(2,1)}), bf16[8,128,1024]{2,1,0:T(8,128)(2,1)}, u32[]{:S(2)}, u32[]{:S(2)}) %all-to-all-start) | async-done | bytes 2097184 | tf_op jit(solution)/shard_map/all_to_all | solution.py:206
  184.9 2.0 convert_bitcast_fusion
  188.7 3.6 %collective-permute-start.29 = (bf16[256,1024]{1,0:T(8,128)(2,1)S(1)}, bf16[256,1024]{1,0:T(8,128)(2,1)S(1)}, u32[]{:S(2)}, u32[]{:S(2)}) collective-permute-start(bf16[256,1024]{1,0:T(8,128)(2,1)S(1)} %pad_maximum_fusion.3), channel_id=1, source_target_pairs={{0,0},{1,8},{2,2},{3,10},{4,4},{5,12},{6,6},{7,14},{8,1},{9,9},{10... | collective-permute-start | bytes 1572872 | tf_op jit(solution)/shard_map/ppermute | solution.py:122
  192.3 1.8 add_convert_fusion
  194.1 5.1 %collective-permute-done.29 = bf16[256,1024]{1,0:T(8,128)(2,1)S(1)} collective-permute-done((bf16[256,1024]{1,0:T(8,128)(2,1)S(1)}, bf16[256,1024]{1,0:T(8,128)(2,1)S(1)}, u32[]{:S(2)}, u32[]{:S(2)}) %collective-permute-start.29) | collective-permute-done | bytes 524320 | tf_op jit(solution)/shard_map/ppermute | solution.py:122
  200.4 1.8 shard_map.71
  (110 shorter events, 20.9 us)
Async XLA Ops:
  7.2 8.0 %copy-start.3 = (bf16[128,8192]{1,0:T(8,128)(2,1)S(1)}, bf16[128,8192]{1,0:T(8,128)(2,1)}, u32[]{:S(2)}) copy-start(bf16[128,8192]{1,0:T(8,128)(2,1)} %cotangent.1) | copy-start | bytes 6291460
  7.2 105.0 %all-gather.2.cloned.1.call-start = ((), (), s32[]{:S(2)}) async-start(), calls=%async_computation.2 | async-start | bytes 9437184 | tf_op jit(solution)/shard_map/all_gather | solution.py:143
  7.3 1.3 copy-start.6
  10.5 188.7 %reduce-scatter.2.cloned.1.call-start = ((), (), s32[]{:S(2)}) async-start(), calls=%async_computation.3 | async-start | bytes 9437184 | tf_op jit(solution)/shard_map/reduce_scatter | solution.py:202
  10.5 12.0 %collective-permute-start = (bf16[256,1024]{1,0:T(8,128)(2,1)}, bf16[256,1024]{1,0:T(8,128)(2,1)S(1)}, u32[]{:S(2)}, u32[]{:S(2)}) collective-permute-start(bf16[256,1024]{1,0:T(8,128)(2,1)} %param.6), channel_id=1, source_target_pairs={{0,0},{1,8},{2,2},{3,10},{4,4},{5,12},{6,6},{7,14},{8,1},{9,9},{10... | collective-permute-start | bytes 1572872 | tf_op jit(solution)/shard_map/ppermute | solution.py:122
  17.7 18.5 %collective-permute-start.3 = (bf16[2,128,1024]{2,1,0:T(8,128)(2,1)}, bf16[2,128,1024]{2,1,0:T(8,128)(2,1)S(1)}, u32[]{:S(2)}, u32[]{:S(2)}) collective-permute-start(bf16[2,128,1024]{2,1,0:T(8,128)(2,1)} %get-tuple-element.106), channel_id=1, source_target_pairs={{0,2},{1,3},{2,4},{3,5},{4,6},{5,7},{6,0},{7,1},{8,14},{9,15},{10,... | collective-permute-start | bytes 1572872 | tf_op jit(solution)/shard_map/ppermute | solution.py:122
  22.5 9.3 %copy-start.12 = (bf16[256,1024]{1,0:T(8,128)(2,1)}, bf16[256,1024]{1,0:T(8,128)(2,1)S(1)}, u32[]{:S(2)}) copy-start(bf16[256,1024]{1,0:T(8,128)(2,1)S(1)} %collective-permute-done) | copy-start | bytes 1572868
  23.4 5.6 %collective-permute-start.1 = (bf16[128,1024]{1,0:T(8,128)(2,1)S(1)}, bf16[128,1024]{1,0:T(8,128)(2,1)S(1)}, u32[]{:S(2)}, u32[]{:S(2)}) collective-permute-start(bf16[128,1024]{1,0:T(8,128)(2,1)S(1)} %get-tuple-element.111), channel_id=1, source_target_pairs={{0,1},{1,64},{2,3},{3,66},{4,5},{5,68},{6,7},{7,70},{8,73},{9,8},{... | collective-permute-start | bytes 786440 | tf_op jit(solution)/shard_map/ppermute | solution.py:122
  23.4 11.2 %collective-permute-start.2 = (bf16[128,1024]{1,0:T(8,128)(2,1)S(1)}, bf16[128,1024]{1,0:T(8,128)(2,1)S(1)}, u32[]{:S(2)}, u32[]{:S(2)}) collective-permute-start(bf16[128,1024]{1,0:T(8,128)(2,1)S(1)} %get-tuple-element.118), channel_id=1, source_target_pairs={{0,16},{1,17},{2,18},{3,19},{4,20},{5,21},{6,22},{7,23},{8,56},{9,... | collective-permute-start | bytes 786440 | tf_op jit(solution)/shard_map/ppermute | solution.py:122
  27.1 13.0 %collective-permute-start.4 = (bf16[128,1024]{1,0:T(8,128)(2,1)S(1)}, bf16[128,1024]{1,0:T(8,128)(2,1)S(1)}, u32[]{:S(2)}, u32[]{:S(2)}) collective-permute-start(bf16[128,1024]{1,0:T(8,128)(2,1)S(1)} %get-tuple-element.111), channel_id=1, source_target_pairs={{0,65},{1,0},{2,67},{3,2},{4,69},{5,4},{6,71},{7,6},{8,9},{9,72},{... | collective-permute-start | bytes 786440 | tf_op jit(solution)/shard_map/ppermute | solution.py:122
  29.0 11.8 %collective-permute-start.5 = (bf16[128,1024]{1,0:T(8,128)(2,1)S(1)}, bf16[128,1024]{1,0:T(8,128)(2,1)S(1)}, u32[]{:S(2)}, u32[]{:S(2)}) collective-permute-start(bf16[128,1024]{1,0:T(8,128)(2,1)S(1)} %get-tuple-element.111), channel_id=1, source_target_pairs={{0,64},{1,65},{2,66},{3,67},{4,68},{5,69},{6,70},{7,71},{8,72},{9,... | collective-permute-start | bytes 786440 | tf_op jit(solution)/shard_map/ppermute | solution.py:122
  31.8 26.6 %collective-permute-start.11 = (bf16[2,128,1024]{2,1,0:T(8,128)(2,1)}, bf16[2,128,1024]{2,1,0:T(8,128)(2,1)S(1)}, u32[]{:S(2)}, u32[]{:S(2)}) collective-permute-start(bf16[2,128,1024]{2,1,0:T(8,128)(2,1)} %get-tuple-element.134), channel_id=1, source_target_pairs={{0,4},{1,5},{2,6},{3,7},{4,0},{5,1},{6,2},{7,3},{8,12},{9,13},{10,... | collective-permute-start | bytes 1572872 | tf_op jit(solution)/shard_map/ppermute | solution.py:122
  34.6 8.6 %copy-start.15 = (bf16[128,1024]{1,0:T(8,128)(2,1)}, bf16[128,1024]{1,0:T(8,128)(2,1)S(1)}, u32[]{:S(2)}) copy-start(bf16[128,1024]{1,0:T(8,128)(2,1)S(1)} %collective-permute-done.2) | copy-start | bytes 786436
  34.6 8.6 %collective-permute-start.6 = (bf16[128,1024]{1,0:T(8,128)(2,1)S(1)}, bf16[128,1024]{1,0:T(8,128)(2,1)S(1)}, u32[]{:S(2)}, u32[]{:S(2)}) collective-permute-start(bf16[128,1024]{1,0:T(8,128)(2,1)S(1)} %get-tuple-element.118), channel_id=1, source_target_pairs={{0,48},{1,49},{2,50},{3,51},{4,52},{5,53},{6,54},{7,55},{8,24},{9,... | collective-permute-start | bytes 786440 | tf_op jit(solution)/shard_map/ppermute | solution.py:122
  36.2 11.1 %collective-permute-start.7 = (bf16[128,1024]{1,0:T(8,128)(2,1)S(1)}, bf16[128,1024]{1,0:T(8,128)(2,1)S(1)}, u32[]{:S(2)}, u32[]{:S(2)}) collective-permute-start(bf16[128,1024]{1,0:T(8,128)(2,1)S(1)} %get-tuple-element.118), channel_id=1, source_target_pairs={{0,32},{1,33},{2,34},{3,35},{4,36},{5,37},{6,38},{7,39},{8,40},{9,... | collective-permute-start | bytes 786440 | tf_op jit(solution)/shard_map/ppermute | solution.py:122
  43.1 7.2 %copy-start.9 = (bf16[2,128,1024]{2,1,0:T(8,128)(2,1)S(1)}, bf16[2,128,1024]{2,1,0:T(8,128)(2,1)}, u32[]{:S(2)}) copy-start(bf16[2,128,1024]{2,1,0:T(8,128)(2,1)} %copy-done.8) | copy-start | bytes 1572868
  43.1 40.7 %copy-start.1 = (bf16[4096,1024]{1,0:T(8,128)(2,1)S(1)}, bf16[4096,1024]{1,0:T(8,128)(2,1)}, u32[]{:S(2)}) copy-start(bf16[4096,1024]{1,0:T(8,128)(2,1)} %get-tuple-element.179) | copy-start | bytes 25165828
  48.4 28.3 %collective-permute-start.10 = (bf16[512,1024]{1,0:T(8,128)(2,1)S(1)}, bf16[512,1024]{1,0:T(8,128)(2,1)S(1)}, u32[]{:S(2)}, u32[]{:S(2)}) collective-permute-start(bf16[512,1024]{1,0:T(8,128)(2,1)S(1)} %pad_maximum_fusion.1), channel_id=1, source_target_pairs={{0,1},{1,64},{2,3},{3,66},{4,5},{5,68},{6,7},{7,70},{8,73},{9,8},{... | collective-permute-start | bytes 3145736 | tf_op jit(solution)/shard_map/ppermute | solution.py:122
  49.0 29.2 %collective-permute-start.9 = (bf16[512,1024]{1,0:T(8,128)(2,1)S(1)}, bf16[512,1024]{1,0:T(8,128)(2,1)S(1)}, u32[]{:S(2)}, u32[]{:S(2)}) collective-permute-start(bf16[512,1024]{1,0:T(8,128)(2,1)S(1)} %pad_maximum_fusion), channel_id=1, source_target_pairs={{0,16},{1,17},{2,18},{3,19},{4,20},{5,21},{6,22},{7,23},{8,56},{9,... | collective-permute-start | bytes 3145736 | tf_op jit(solution)/shard_map/ppermute | solution.py:122
  50.3 24.3 %collective-permute-start.8 = (bf16[2,128,1024]{2,1,0:T(8,128)(2,1)S(1)}, bf16[2,128,1024]{2,1,0:T(8,128)(2,1)S(1)}, u32[]{:S(2)}, u32[]{:S(2)}) collective-permute-start(bf16[2,128,1024]{2,1,0:T(8,128)(2,1)S(1)} %copy-done.9), channel_id=1, source_target_pairs={{0,6},{1,7},{2,0},{3,1},{4,2},{5,3},{6,4},{7,5},{8,10},{9,11},{10,... | collective-permute-start | bytes 1572872 | tf_op jit(solution)/shard_map/ppermute | solution.py:122
  58.4 16.2 %copy-start.4 = (bf16[2,128,1024]{2,1,0:T(8,128)(2,1)}, bf16[2,128,1024]{2,1,0:T(8,128)(2,1)S(1)}, u32[]{:S(2)}) copy-start(bf16[2,128,1024]{2,1,0:T(8,128)(2,1)S(1)} %collective-permute-done.11.across) | copy-start | bytes 1572868
  58.5 25.3 %collective-permute-start.12 = (bf16[512,1024]{1,0:T(8,128)(2,1)S(1)}, bf16[512,1024]{1,0:T(8,128)(2,1)S(1)}, u32[]{:S(2)}, u32[]{:S(2)}) collective-permute-start(bf16[512,1024]{1,0:T(8,128)(2,1)S(1)} %pad_maximum_fusion), channel_id=1, source_target_pairs={{0,48},{1,49},{2,50},{3,51},{4,52},{5,53},{6,54},{7,55},{8,24},{9,... | collective-permute-start | bytes 3145736 | tf_op jit(solution)/shard_map/ppermute | solution.py:122
  59.3 24.5 %collective-permute-start.13 = (bf16[512,1024]{1,0:T(8,128)(2,1)S(1)}, bf16[512,1024]{1,0:T(8,128)(2,1)S(1)}, u32[]{:S(2)}, u32[]{:S(2)}) collective-permute-start(bf16[512,1024]{1,0:T(8,128)(2,1)S(1)} %pad_maximum_fusion.1), channel_id=1, source_target_pairs={{0,65},{1,0},{2,67},{3,2},{4,69},{5,4},{6,71},{7,6},{8,9},{9,72},{... | collective-permute-start | bytes 3145736 | tf_op jit(solution)/shard_map/ppermute | solution.py:122
  74.7 9.5 %collective-permute-start.14 = (bf16[512,1024]{1,0:T(8,128)(2,1)S(1)}, bf16[512,1024]{1,0:T(8,128)(2,1)S(1)}, u32[]{:S(2)}, u32[]{:S(2)}) collective-permute-start(bf16[512,1024]{1,0:T(8,128)(2,1)S(1)} %pad_maximum_fusion.2), channel_id=1, source_target_pairs={{0,8},{1,9},{2,10},{3,11},{4,12},{5,13},{6,14},{7,15},{8,0},{9,1},... | collective-permute-start | bytes 3145736 | tf_op jit(solution)/shard_map/ppermute | solution.py:122
  76.6 7.6 %copy-start.5 = (bf16[2,128,1024]{2,1,0:T(8,128)(2,1)S(1)}, bf16[2,128,1024]{2,1,0:T(8,128)(2,1)}, u32[]{:S(2)}) copy-start(bf16[2,128,1024]{2,1,0:T(8,128)(2,1)} %copy-done.4) | copy-start | bytes 1572868
  76.7 15.7 %collective-permute-start.16 = (bf16[512,1024]{1,0:T(8,128)(2,1)S(1)}, bf16[512,1024]{1,0:T(8,128)(2,1)S(1)}, u32[]{:S(2)}, u32[]{:S(2)}) collective-permute-start(bf16[512,1024]{1,0:T(8,128)(2,1)S(1)} %collective-permute-done.10), channel_id=1, source_target_pairs={{0,1},{1,64},{2,3},{3,66},{4,5},{5,68},{6,7},{7,70},{8,73},{9,8},{... | collective-permute-start | bytes 3145736 | tf_op jit(solution)/shard_map/ppermute | solution.py:122
  78.2 17.4 %collective-permute-start.15 = (bf16[512,1024]{1,0:T(8,128)(2,1)S(1)}, bf16[512,1024]{1,0:T(8,128)(2,1)S(1)}, u32[]{:S(2)}, u32[]{:S(2)}) collective-permute-start(bf16[512,1024]{1,0:T(8,128)(2,1)S(1)} %collective-permute-done.9), channel_id=1, source_target_pairs={{0,16},{1,17},{2,18},{3,19},{4,20},{5,21},{6,22},{7,23},{8,56},{9,... | collective-permute-start | bytes 3145736 | tf_op jit(solution)/shard_map/ppermute | solution.py:122
  108.8 3.3 %copy-start.2 = (bf16[4096,1024]{1,0:T(8,128)(2,1)}, bf16[4096,1024]{1,0:T(8,128)(2,1)S(1)}, u32[]{:S(2)}) copy-start(bf16[4096,1024]{1,0:T(8,128)(2,1)S(1)} %select_dynamic-update-slice_fusion.refs_0_) | copy-start | bytes 25165828
  112.2 9.9 %copy-start.10 = (bf16[1024,4096]{1,0:T(8,128)(2,1)S(1)}, bf16[1024,4096]{1,0:T(8,128)(2,1)}, u32[]{:S(2)}) copy-start(bf16[1024,4096]{1,0:T(8,128)(2,1)} %all-gather.2.cloned.1.call-done) | copy-start | bytes 25165828
  112.2 11.2 %slice-start = ((s8[8388608]{0:T(1024)(128)(4,1)}), s8[4194304]{0:T(1024)(128)(4,1)S(1)}, s32[]{:S(2)}) async-start(s8[8388608]{0:T(1024)(128)(4,1)} %bitcast.30), calls=%async_computation.4 | async-start | bytes 8388608
  114.9 8.5 %slice-start.1 = ((s8[8388608]{0:T(1024)(128)(4,1)}), s8[4194304]{0:T(1024)(128)(4,1)S(1)}, s32[]{:S(2)}) async-start(s8[8388608]{0:T(1024)(128)(4,1)} %bitcast.30), calls=%async_computation.5 | async-start | bytes 8388608
  114.9 21.1 %collective-permute-start.23 = (bf16[512,1024]{1,0:T(8,128)(2,1)S(1)}, bf16[512,1024]{1,0:T(8,128)(2,1)S(1)}, u32[]{:S(2)}, u32[]{:S(2)}) collective-permute-start(bf16[512,1024]{1,0:T(8,128)(2,1)S(1)} %multiply_convert_fusion.6.refs_2_), channel_id=1, source_target_pairs={{0,65},{1,0},{2,67},{3,2},{4,69},{5,4},{6,71},{7,6},{8,9},{9,72},{... | collective-permute-start | bytes 3145736 | tf_op jit(solution)/shard_map/ppermute | solution.py:122
  118.3 23.5 %collective-permute-start.18 = (bf16[512,1024]{1,0:T(8,128)(2,1)S(1)}, bf16[512,1024]{1,0:T(8,128)(2,1)S(1)}, u32[]{:S(2)}, u32[]{:S(2)}) collective-permute-start(bf16[512,1024]{1,0:T(8,128)(2,1)S(1)} %multiply_convert_fusion.7.refs_1_), channel_id=1, source_target_pairs={{0,48},{1,49},{2,50},{3,51},{4,52},{5,53},{6,54},{7,55},{8,24},{9,... | collective-permute-start | bytes 3145736 | tf_op jit(solution)/shard_map/ppermute | solution.py:122
  132.5 9.3 %copy-start = (bf16[1024,1024]{1,0:T(8,128)(2,1)}, bf16[1024,1024]{1,0:T(8,128)(2,1)S(1)}, u32[]{:S(2)}) copy-start(bf16[1024,1024]{1,0:T(8,128)(2,1)S(1)} %convolution_convert_fusion.1.refs_1_) | copy-start | bytes 6291460
  132.5 25.4 %collective-permute-start.22 = (bf16[512,1024]{1,0:T(8,128)(2,1)}, bf16[512,1024]{1,0:T(8,128)(2,1)}, u32[]{:S(2)}, u32[]{:S(2)}) collective-permute-start(bf16[512,1024]{1,0:T(8,128)(2,1)} %multiply_convert_fusion.4.refs_4_), channel_id=1, source_target_pairs={{0,1},{1,64},{2,3},{3,66},{4,5},{5,68},{6,7},{7,70},{8,73},{9,8},{... | collective-permute-start | bytes 3145736 | tf_op jit(solution)/shard_map/ppermute | solution.py:122
  137.5 26.4 %collective-permute-start.24 = (bf16[512,1024]{1,0:T(8,128)(2,1)}, bf16[512,1024]{1,0:T(8,128)(2,1)}, u32[]{:S(2)}, u32[]{:S(2)}) collective-permute-start(bf16[512,1024]{1,0:T(8,128)(2,1)} %add_convert_fusion.2), channel_id=1, source_target_pairs={{0,65},{1,0},{2,67},{3,2},{4,69},{5,4},{6,71},{7,6},{8,9},{9,72},{... | collective-permute-start | bytes 3145736 | tf_op jit(solution)/shard_map/ppermute | solution.py:122
  138.8 27.5 %collective-permute-start.17 = (bf16[512,1024]{1,0:T(8,128)(2,1)S(1)}, bf16[512,1024]{1,0:T(8,128)(2,1)}, u32[]{:S(2)}, u32[]{:S(2)}) collective-permute-start(bf16[512,1024]{1,0:T(8,128)(2,1)S(1)} %multiply_convert_fusion.5.refs_3_), channel_id=1, source_target_pairs={{0,16},{1,17},{2,18},{3,19},{4,20},{5,21},{6,22},{7,23},{8,56},{9,... | collective-permute-start | bytes 3145736 | tf_op jit(solution)/shard_map/ppermute | solution.py:122
  143.2 25.6 %collective-permute-start.19 = (bf16[512,1024]{1,0:T(8,128)(2,1)}, bf16[512,1024]{1,0:T(8,128)(2,1)}, u32[]{:S(2)}, u32[]{:S(2)}) collective-permute-start(bf16[512,1024]{1,0:T(8,128)(2,1)} %add_convert_fusion.4), channel_id=1, source_target_pairs={{0,48},{1,49},{2,50},{3,51},{4,52},{5,53},{6,54},{7,55},{8,24},{9,... | collective-permute-start | bytes 3145736 | tf_op jit(solution)/shard_map/ppermute | solution.py:122
  145.5 39.4 %all-to-all-start = ((bf16[8,128,1024]{2,1,0:T(8,128)(2,1)}), bf16[8,128,1024]{2,1,0:T(8,128)(2,1)}, u32[]{:S(2)}, u32[]{:S(2)}) async-start(bf16[8,128,1024]{2,1,0:T(8,128)(2,1)} %bitcast.29), calls=%async_computation | async-start | bytes 4194304 | tf_op jit(solution)/shard_map/all_to_all | solution.py:206
  155.2 8.6 %copy-start.14 = (bf16[512,1024]{1,0:T(8,128)(2,1)S(1)}, bf16[512,1024]{1,0:T(8,128)(2,1)}, u32[]{:S(2)}) copy-start(bf16[512,1024]{1,0:T(8,128)(2,1)} %multiply_convert_fusion.1) | copy-start | bytes 3145732
  165.9 9.2 %collective-permute-start.25 = (bf16[128,1024]{1,0:T(8,128)(2,1)S(1)}, bf16[128,1024]{1,0:T(8,128)(2,1)S(1)}, u32[]{:S(2)}, u32[]{:S(2)}) collective-permute-start(bf16[128,1024]{1,0:T(8,128)(2,1)S(1)} %get-tuple-element.185), channel_id=1, source_target_pairs={{0,48},{1,49},{2,50},{3,51},{4,52},{5,53},{6,54},{7,55},{8,24},{9,... | collective-permute-start | bytes 786440 | tf_op jit(solution)/shard_map/ppermute | solution.py:122
  170.9 7.6 %collective-permute-start.20 = (bf16[128,1024]{1,0:T(8,128)(2,1)S(1)}, bf16[128,1024]{1,0:T(8,128)(2,1)S(1)}, u32[]{:S(2)}, u32[]{:S(2)}) collective-permute-start(bf16[128,1024]{1,0:T(8,128)(2,1)S(1)} %get-tuple-element.184), channel_id=1, source_target_pairs={{0,65},{1,0},{2,67},{3,2},{4,69},{5,4},{6,71},{7,6},{8,9},{9,72},{... | collective-permute-start | bytes 786440 | tf_op jit(solution)/shard_map/ppermute | solution.py:122
  171.7 15.6 %collective-permute-start.27 = (bf16[128,1024]{1,0:T(8,128)(2,1)S(1)}, bf16[128,1024]{1,0:T(8,128)(2,1)S(1)}, u32[]{:S(2)}, u32[]{:S(2)}) collective-permute-start(bf16[128,1024]{1,0:T(8,128)(2,1)S(1)} %get-tuple-element.183), channel_id=1, source_target_pairs={{0,1},{1,64},{2,3},{3,66},{4,5},{5,68},{6,7},{7,70},{8,73},{9,8},{... | collective-permute-start | bytes 786440 | tf_op jit(solution)/shard_map/ppermute | solution.py:122
  173.6 13.7 %collective-permute-start.28 = (bf16[128,1024]{1,0:T(8,128)(2,1)S(1)}, bf16[128,1024]{1,0:T(8,128)(2,1)S(1)}, u32[]{:S(2)}, u32[]{:S(2)}) collective-permute-start(bf16[128,1024]{1,0:T(8,128)(2,1)S(1)} %get-tuple-element.186), channel_id=1, source_target_pairs={{0,16},{1,17},{2,18},{3,19},{4,20},{5,21},{6,22},{7,23},{8,56},{9,... | collective-permute-start | bytes 786440 | tf_op jit(solution)/shard_map/ppermute | solution.py:122
  175.9 11.4 %collective-permute-start.26 = (bf16[128,1024]{1,0:T(8,128)(2,1)}, bf16[128,1024]{1,0:T(8,128)(2,1)}, u32[]{:S(2)}, u32[]{:S(2)}) collective-permute-start(bf16[128,1024]{1,0:T(8,128)(2,1)} %add_convert_fusion.7), channel_id=1, source_target_pairs={{0,48},{1,49},{2,50},{3,51},{4,52},{5,53},{6,54},{7,55},{8,24},{9,... | collective-permute-start | bytes 786440 | tf_op jit(solution)/shard_map/ppermute | solution.py:122
  179.3 8.0 %collective-permute-start.21 = (bf16[128,1024]{1,0:T(8,128)(2,1)}, bf16[128,1024]{1,0:T(8,128)(2,1)S(1)}, u32[]{:S(2)}, u32[]{:S(2)}) collective-permute-start(bf16[128,1024]{1,0:T(8,128)(2,1)} %add_convert_fusion.8), channel_id=1, source_target_pairs={{0,65},{1,0},{2,67},{3,2},{4,69},{5,4},{6,71},{7,6},{8,9},{9,72},{... | collective-permute-start | bytes 786440 | tf_op jit(solution)/shard_map/ppermute | solution.py:122
  187.3 5.1 %copy-start.11 = (bf16[128,8192]{1,0:T(8,128)(2,1)S(1)}, bf16[128,8192]{1,0:T(8,128)(2,1)}, u32[]{:S(2)}) copy-start(bf16[128,8192]{1,0:T(8,128)(2,1)} %param.5) | copy-start | bytes 6291460
  188.7 10.5 %collective-permute-start.29 = (bf16[256,1024]{1,0:T(8,128)(2,1)S(1)}, bf16[256,1024]{1,0:T(8,128)(2,1)S(1)}, u32[]{:S(2)}, u32[]{:S(2)}) collective-permute-start(bf16[256,1024]{1,0:T(8,128)(2,1)S(1)} %pad_maximum_fusion.3), channel_id=1, source_target_pairs={{0,0},{1,8},{2,2},{3,10},{4,4},{5,12},{6,6},{7,14},{8,1},{9,9},{10... | collective-permute-start | bytes 1572872 | tf_op jit(solution)/shard_map/ppermute | solution.py:122
  (3 other events, 3.1 us)
Sparse Core Ops, SparseCore 0:
  10.6 70.1 all-gather.1
  112.2 56.8 reduce-scatter.1
